TPU v7x, 512 devices: a whole 4x4x16 slice. The times are simulated.
512 devices in a mesh: dom: 64 (over z_lo, x, core), rep: 8 (over z_hi, y).
Axes of the slice: x: 4, y: 4, z: 16 (z_hi: 2, z_lo: 8; z = z_hi * 8 + z_lo), core: 2. Of those that a mesh axis runs over, the one named last changes fastest.
Arguments:
- features: bfloat16 [65536, 512], P('dom'), may hold values from -6 to 6
- tiles: bfloat16 [24576, 128, 128], P(('dom', 'rep')), may hold values from -0.078125 to 0.078125
- tile_rows: int32 [24576], P(('dom', 'rep')), may hold values from 0 to 7
- tile_cols: int32 [24576], P(('dom', 'rep')), may hold values from 0 to 511, as said below
- tile_count: int32 [512], P(('dom', 'rep')), may hold values from 6 to 48, as said below
- weight: bfloat16 [512, 512], replicated, may hold values from -0.25 to 0.25
- cotangent: bfloat16 [65536, 512], P(('dom', 'rep')), may hold values from -6 to 6
Outputs:
- node_out: bfloat16 [65536, 512], P(('dom', 'rep'))
- weight_grad: float32 [512, 512], replicated
Inputs may be any that keep to these rules, and one draw needn't show every extreme that they name: Each device holds distinct (tile_rows, tile_cols) pairs; the slots of device d = p * 8 + r name tile columns of the 8 partitions q with (p - r - q) mod 64 divisible by 8. `tile_count`: some device uses all its slots.
All inputs are finite; a program needn't handle non-finite values.
Results may differ from a plain program's by a relative error of at most 0.015.
Values may be sent and summed in bfloat16 or wider, within the bound.
A program may use at most 64 MiB of HBM per device.

v0:
```python
import jax
import jax.numpy as jnp
from jax import lax
from jax.sharding import PartitionSpec as P

slot_span = 16


def from_behind(block, axis, distance):
    devices = range(lax.axis_size(axis))
    route = [((i - distance) % len(devices), i) for i in devices]
    return lax.ppermute(block, axis, route)


def shards(features, tiles, tile_rows, tile_cols, tile_count, weight, cotangent):
    dom_size = lax.axis_size("dom")
    rep_size = lax.axis_size("rep")
    source_steps = dom_size // rep_size
    owner = lax.axis_index("dom")
    member = lax.axis_index("rep")
    tile_size = tiles.shape[1]
    feature_width = features.shape[1]
    row_tiles = features.shape[0] // tile_size
    travelling = features
    held_block = features
    for hop_number in range(1, rep_size):
        travelling = from_behind(travelling, "dom", 1)
        held_block = jnp.where(member == hop_number, travelling, held_block)
    received = [held_block] * source_steps
    ahead = held_block
    for ahead_step in range(1, source_steps):
        ahead = from_behind(ahead, "dom", rep_size)
        received[ahead_step] = ahead
    buffer = jnp.stack(received).reshape(source_steps * row_tiles, tile_size, feature_width)
    live_count = tile_count[0]
    source = tile_cols // row_tiles
    column = tile_cols % row_tiles
    source_step = (owner - member - source) % dom_size // rep_size
    input_index = source_step * row_tiles + column
    block_total = (live_count + slot_span - 1) // slot_span
    tile_order = jnp.arange(row_tiles)

    def one_block(block_index, totals):
        start = block_index * slot_span
        tile_block = lax.dynamic_slice_in_dim(tiles, start, slot_span, 0)
        index_block = lax.dynamic_slice_in_dim(input_index, start, slot_span, 0)
        row_block = lax.dynamic_slice_in_dim(tile_rows, start, slot_span, 0)
        live_slots = start + jnp.arange(slot_span) < live_count
        inputs = buffer[index_block]
        products = jnp.einsum(
            "sij,sjf->sif", tile_block, inputs, preferred_element_type=jnp.float32
        )
        placing = ((row_block[:, None] == tile_order[None, :]) & live_slots[:, None]).astype(
            jnp.float32
        )
        return totals + jnp.einsum("st,sif->tif", placing, products)

    totals = jnp.zeros((row_tiles, tile_size, feature_width), jnp.float32)
    totals = lax.fori_loop(0, block_total, one_block, totals)
    partial_rows = totals.reshape(row_tiles * tile_size, feature_width)
    aggregate = lax.psum_scatter(partial_rows, "rep", scatter_dimension=0, tiled=True)
    aggregated = aggregate.astype(jnp.bfloat16)
    pre = jnp.dot(aggregated, weight, preferred_element_type=jnp.float32)
    sigma = jax.nn.sigmoid(pre)
    node_out = (pre * sigma).astype(jnp.bfloat16)
    slope = (cotangent.astype(jnp.float32) * sigma * (1.0 + pre * (1.0 - sigma))).astype(
        jnp.bfloat16
    )
    local_grad = jnp.einsum("nf,ng->fg", aggregated, slope, preferred_element_type=jnp.float32)
    weight_grad = lax.psum(local_grad, ("dom", "rep"))
    return (node_out, weight_grad)


def solution(mesh):
    in_specs = (
        P("dom", None),
        P(("dom", "rep"), None, None),
        P(("dom", "rep")),
        P(("dom", "rep")),
        P(("dom", "rep")),
        P(),
        P(("dom", "rep"), None),
    )
    out_specs = (P(("dom", "rep"), None), P())
    return jax.shard_map(shards, mesh=mesh, in_specs=in_specs, out_specs=out_specs, check_vma=False)
```

profile of v0, /device:TPU:1, one launch (start us, length us, event | category | flops | bytes accessed | tf_op | source)
XLA Modules:
  0.0 1040.1 jit_solution(14774627038103160619)
XLA Ops:
  7.2 4.6 collective-permute-start
  11.9 12.0 %collective-permute-done = bf16[1024,512]{1,0:T(8,128)(2,1)S(1)} collective-permute-done((bf16[1024,512]{1,0:T(8,128)(2,1)}, bf16[1024,512]{1,0:T(8,128)(2,1)S(1)}, u32[]{:S(2)}, u32[]{:S(2)}) %collective-permute-start) | collective-permute-done | bytes 1048608 | tf_op jit(solution)/shard_map/ppermute | solution.py:12
  23.9 4.3 collective-permute-start.1
  28.2 15.1 %collective-permute-done.1 = bf16[1024,512]{1,0:T(8,128)(2,1)S(1)} collective-permute-done((bf16[1024,512]{1,0:T(8,128)(2,1)S(1)}, bf16[1024,512]{1,0:T(8,128)(2,1)S(1)}, u32[]{:S(2)}, u32[]{:S(2)}) %collective-permute-start.1) | collective-permute-done | bytes 1048608 | tf_op jit(solution)/shard_map/ppermute | solution.py:12
  45.2 22.9 %collective-permute-done.2 = bf16[1024,512]{1,0:T(8,128)(2,1)S(1)} collective-permute-done((bf16[1024,512]{1,0:T(8,128)(2,1)S(1)}, bf16[1024,512]{1,0:T(8,128)(2,1)S(1)}, u32[]{:S(2)}, u32[]{:S(2)}) %collective-permute-start.2) | collective-permute-done | bytes 1048608 | tf_op jit(solution)/shard_map/ppermute | solution.py:12
  71.1 22.9 %collective-permute-done.3 = bf16[1024,512]{1,0:T(8,128)(2,1)S(1)} collective-permute-done((bf16[1024,512]{1,0:T(8,128)(2,1)S(1)}, bf16[1024,512]{1,0:T(8,128)(2,1)S(1)}, u32[]{:S(2)}, u32[]{:S(2)}) %collective-permute-start.3) | collective-permute-done | bytes 1048608 | tf_op jit(solution)/shard_map/ppermute | solution.py:12
  96.9 22.9 %collective-permute-done.4 = bf16[1024,512]{1,0:T(8,128)(2,1)S(1)} collective-permute-done((bf16[1024,512]{1,0:T(8,128)(2,1)S(1)}, bf16[1024,512]{1,0:T(8,128)(2,1)S(1)}, u32[]{:S(2)}, u32[]{:S(2)}) %collective-permute-start.4) | collective-permute-done | bytes 1048608 | tf_op jit(solution)/shard_map/ppermute | solution.py:12
  122.7 23.0 %collective-permute-done.5 = bf16[1024,512]{1,0:T(8,128)(2,1)} collective-permute-done((bf16[1024,512]{1,0:T(8,128)(2,1)S(1)}, bf16[1024,512]{1,0:T(8,128)(2,1)}, u32[]{:S(2)}, u32[]{:S(2)}) %collective-permute-start.5) | collective-permute-done | bytes 1048608 | tf_op jit(solution)/shard_map/ppermute | solution.py:12
  145.7 1.9 collective-permute-start.6
  147.6 23.2 %collective-permute-done.6 = bf16[1024,512]{1,0:T(8,128)(2,1)} collective-permute-done((bf16[1024,512]{1,0:T(8,128)(2,1)}, bf16[1024,512]{1,0:T(8,128)(2,1)}, u32[]{:S(2)}, u32[]{:S(2)}) %collective-permute-start.6) | collective-permute-done | bytes 1048608 | tf_op jit(solution)/shard_map/ppermute | solution.py:12
  170.8 3.3 bitcast_dynamic-update-slice_fusion.7
  176.1 20.6 %collective-permute-done.7 = bf16[1024,512]{1,0:T(8,128)(2,1)S(1)} collective-permute-done((bf16[1024,512]{1,0:T(8,128)(2,1)S(1)}, bf16[1024,512]{1,0:T(8,128)(2,1)S(1)}, u32[]{:S(2)}, u32[]{:S(2)}) %collective-permute-start.7) | collective-permute-done | bytes 1048608 | tf_op jit(solution)/shard_map/ppermute | solution.py:12
  198.6 24.7 %collective-permute-done.8 = bf16[1024,512]{1,0:T(8,128)(2,1)S(1)} collective-permute-done((bf16[1024,512]{1,0:T(8,128)(2,1)S(1)}, bf16[1024,512]{1,0:T(8,128)(2,1)S(1)}, u32[]{:S(2)}, u32[]{:S(2)}) %collective-permute-start.8) | collective-permute-done | bytes 1048608 | tf_op jit(solution)/shard_map/ppermute | solution.py:12
  225.3 23.8 %collective-permute-done.9 = bf16[1024,512]{1,0:T(8,128)(2,1)S(1)} collective-permute-done((bf16[1024,512]{1,0:T(8,128)(2,1)S(1)}, bf16[1024,512]{1,0:T(8,128)(2,1)S(1)}, u32[]{:S(2)}, u32[]{:S(2)}) %collective-permute-start.9) | collective-permute-done | bytes 1048608 | tf_op jit(solution)/shard_map/ppermute | solution.py:12
  251.0 22.9 %collective-permute-done.10 = bf16[1024,512]{1,0:T(8,128)(2,1)S(1)} collective-permute-done((bf16[1024,512]{1,0:T(8,128)(2,1)S(1)}, bf16[1024,512]{1,0:T(8,128)(2,1)S(1)}, u32[]{:S(2)}, u32[]{:S(2)}) %collective-permute-start.10) | collective-permute-done | bytes 1048608 | tf_op jit(solution)/shard_map/ppermute | solution.py:12
  273.9 1.9 collective-permute-start.11
  275.8 21.9 %collective-permute-done.11 = bf16[1024,512]{1,0:T(8,128)(2,1)} collective-permute-done((bf16[1024,512]{1,0:T(8,128)(2,1)S(1)}, bf16[1024,512]{1,0:T(8,128)(2,1)}, u32[]{:S(2)}, u32[]{:S(2)}) %collective-permute-start.11) | collective-permute-done | bytes 1048608 | tf_op jit(solution)/shard_map/ppermute | solution.py:12
  297.7 1.9 collective-permute-start.12
  301.4 2.3 bitcast_dynamic-update-slice_fusion.5
  303.7 17.5 %collective-permute-done.12 = bf16[1024,512]{1,0:T(8,128)(2,1)} collective-permute-done((bf16[1024,512]{1,0:T(8,128)(2,1)}, bf16[1024,512]{1,0:T(8,128)(2,1)}, u32[]{:S(2)}, u32[]{:S(2)}) %collective-permute-start.12) | collective-permute-done | bytes 1048608 | tf_op jit(solution)/shard_map/ppermute | solution.py:12
  324.2 2.3 bitcast_dynamic-update-slice_fusion.3
  326.5 2.3 bitcast_dynamic-update-slice_fusion.2
  328.7 2.2 bitcast_dynamic-update-slice_fusion.1
  331.0 12.6 %collective-permute-done.13 = bf16[1024,512]{1,0:T(8,128)(2,1)S(1)} collective-permute-done((bf16[1024,512]{1,0:T(8,128)(2,1)}, bf16[1024,512]{1,0:T(8,128)(2,1)S(1)}, u32[]{:S(2)}, u32[]{:S(2)}) %collective-permute-start.13) | collective-permute-done | bytes 1048608 | tf_op jit(solution)/shard_map/ppermute | solution.py:12
  346.4 10.9 %while.11 = (s32[]{:T(128)}, f32[8,128,512]{2,0,1:T(8,128)}, s32[]{:T(128)}, s32[48]{0:T(128)S(1)}, s32[]{:T(128)}, /*index=5*/bf16[48,128,128]{2,1,0:T(8,128)(2...) while((s32[]{:T(128)}, f32[8,128,512]{2,0,1:T(8,128)}, ...), condition=%wide.region_1.2_spmd.clone, body=%wide.region_0.1_spmd.clone.sunk | while | flops 285738336 | bytes 15209111 | solution.py:59
  346.5 4.1 gather_fusion
  353.0 4.3 fusion.36
  357.3 4.1 copy.9
  361.5 203.2 %reduce-scatter.2.cloned.1.call-done = f32[128,512]{1,0:T(8,128)} async-done(((f32[1024,512]{1,0:T(8,128)}), f32[128,512]{1,0:T(8,128)}) %reduce-scatter.2.cloned.1.call-update) | async-done | bytes 262160 | tf_op jit(solution)/shard_map/reduce_scatter | solution.py:61
  566.6 2.3 fusion.15
  569.0 462.0 %all-reduce.2.cloned.1.call-done = f32[512,512]{1,0:T(8,128)} async-done(((f32[512,512]{1,0:T(8,128)}), f32[512,512]{1,0:T(8,128)}) %all-reduce.2.cloned.1.call-update) | async-done | bytes 1048592 | tf_op jit(solution)/shard_map/psum | solution.py:70
  1031.0 2.3 copy.32
  (42 shorter events, 29.6 us)
Async XLA Ops:
  7.2 557.6 %copy-start = (bf16[512,512]{1,0:T(8,128)(2,1)S(1)}, bf16[512,512]{1,0:T(8,128)(2,1)}, u32[]{:S(2)}) copy-start(bf16[512,512]{1,0:T(8,128)(2,1)} %param.14) | copy-start | bytes 1572868
  7.2 293.2 %copy-start.7 = (s32[48]{0:T(128)S(1)}, s32[48]{0:T(128)}, u32[]{:S(2)}) copy-start(s32[48]{0:T(128)} %param.12) | copy-start | bytes 580
  7.2 557.6 %reduce-scatter.2.cloned.1.call-start = ((), (), s32[]{:S(2)}) async-start(), calls=%async_computation.1 | async-start | bytes 2359296 | tf_op jit(solution)/shard_map/reduce_scatter | solution.py:61
  7.2 16.7 %collective-permute-start = (bf16[1024,512]{1,0:T(8,128)(2,1)}, bf16[1024,512]{1,0:T(8,128)(2,1)S(1)}, u32[]{:S(2)}, u32[]{:S(2)}) collective-permute-start(bf16[1024,512]{1,0:T(8,128)(2,1)} %param.9), channel_id=1, source_target_pairs={{504,0},{0,8},{8,16},{16,24},{24,32},{32,40},{40,48},{48,56},{56,6... | collective-permute-start | bytes 3145736 | tf_op jit(solution)/shard_map/ppermute | solution.py:12
  23.9 19.4 %collective-permute-start.1 = (bf16[1024,512]{1,0:T(8,128)(2,1)S(1)}, bf16[1024,512]{1,0:T(8,128)(2,1)S(1)}, u32[]{:S(2)}, u32[]{:S(2)}) collective-permute-start(bf16[1024,512]{1,0:T(8,128)(2,1)S(1)} %collective-permute-done), channel_id=1, source_target_pairs={{504,0},{0,8},{8,16},{16,24},{24,32},{32,40},{40,48},{48,56},{56,6... | collective-permute-start | bytes 3145736 | tf_op jit(solution)/shard_map/ppermute | solution.py:12
  43.3 24.8 %collective-permute-start.2 = (bf16[1024,512]{1,0:T(8,128)(2,1)S(1)}, bf16[1024,512]{1,0:T(8,128)(2,1)S(1)}, u32[]{:S(2)}, u32[]{:S(2)}) collective-permute-start(bf16[1024,512]{1,0:T(8,128)(2,1)S(1)} %collective-permute-done.1), channel_id=1, source_target_pairs={{504,0},{0,8},{8,16},{16,24},{24,32},{32,40},{40,48},{48,56},{56,6... | collective-permute-start | bytes 3145736 | tf_op jit(solution)/shard_map/ppermute | solution.py:12
  68.2 1.0 copy-start.1
  69.1 24.8 %collective-permute-start.3 = (bf16[1024,512]{1,0:T(8,128)(2,1)S(1)}, bf16[1024,512]{1,0:T(8,128)(2,1)S(1)}, u32[]{:S(2)}, u32[]{:S(2)}) collective-permute-start(bf16[1024,512]{1,0:T(8,128)(2,1)S(1)} %collective-permute-done.2), channel_id=1, source_target_pairs={{504,0},{0,8},{8,16},{16,24},{24,32},{32,40},{40,48},{48,56},{56,6... | collective-permute-start | bytes 3145736 | tf_op jit(solution)/shard_map/ppermute | solution.py:12
  94.0 1.0 copy-start.2
  95.0 24.8 %collective-permute-start.4 = (bf16[1024,512]{1,0:T(8,128)(2,1)S(1)}, bf16[1024,512]{1,0:T(8,128)(2,1)S(1)}, u32[]{:S(2)}, u32[]{:S(2)}) collective-permute-start(bf16[1024,512]{1,0:T(8,128)(2,1)S(1)} %collective-permute-done.3), channel_id=1, source_target_pairs={{504,0},{0,8},{8,16},{16,24},{24,32},{32,40},{40,48},{48,56},{56,6... | collective-permute-start | bytes 3145736 | tf_op jit(solution)/shard_map/ppermute | solution.py:12
  119.8 1.0 copy-start.3
  120.7 25.0 %collective-permute-start.5 = (bf16[1024,512]{1,0:T(8,128)(2,1)S(1)}, bf16[1024,512]{1,0:T(8,128)(2,1)}, u32[]{:S(2)}, u32[]{:S(2)}) collective-permute-start(bf16[1024,512]{1,0:T(8,128)(2,1)S(1)} %collective-permute-done.4), channel_id=1, source_target_pairs={{504,0},{0,8},{8,16},{16,24},{24,32},{32,40},{40,48},{48,56},{56,6... | collective-permute-start | bytes 3145736 | tf_op jit(solution)/shard_map/ppermute | solution.py:12
  145.7 25.1 %collective-permute-start.6 = (bf16[1024,512]{1,0:T(8,128)(2,1)}, bf16[1024,512]{1,0:T(8,128)(2,1)}, u32[]{:S(2)}, u32[]{:S(2)}) collective-permute-start(bf16[1024,512]{1,0:T(8,128)(2,1)} %collective-permute-done.5), channel_id=1, source_target_pairs={{504,0},{0,8},{8,16},{16,24},{24,32},{32,40},{40,48},{48,56},{56,6... | collective-permute-start | bytes 3145736 | tf_op jit(solution)/shard_map/ppermute | solution.py:12
  174.2 22.5 %collective-permute-start.7 = (bf16[1024,512]{1,0:T(8,128)(2,1)S(1)}, bf16[1024,512]{1,0:T(8,128)(2,1)S(1)}, u32[]{:S(2)}, u32[]{:S(2)}) collective-permute-start(bf16[1024,512]{1,0:T(8,128)(2,1)S(1)} %get-tuple-element.87), channel_id=1, source_target_pairs={{448,0},{456,8},{464,16},{472,24},{480,32},{488,40},{496,48},{504,... | collective-permute-start | bytes 3145736 | tf_op jit(solution)/shard_map/ppermute | solution.py:12
  196.7 26.6 %collective-permute-start.8 = (bf16[1024,512]{1,0:T(8,128)(2,1)S(1)}, bf16[1024,512]{1,0:T(8,128)(2,1)S(1)}, u32[]{:S(2)}, u32[]{:S(2)}) collective-permute-start(bf16[1024,512]{1,0:T(8,128)(2,1)S(1)} %collective-permute-done.7), channel_id=1, source_target_pairs={{448,0},{456,8},{464,16},{472,24},{480,32},{488,40},{496,48},{504,... | collective-permute-start | bytes 3145736 | tf_op jit(solution)/shard_map/ppermute | solution.py:12
  223.4 50.5 %copy-start.4 = (bf16[1024,512]{1,0:T(8,128)(2,1)}, bf16[1024,512]{1,0:T(8,128)(2,1)S(1)}, u32[]{:S(2)}) copy-start(bf16[1024,512]{1,0:T(8,128)(2,1)S(1)} %collective-permute-done.8) | copy-start | bytes 3145732
  223.4 25.7 %collective-permute-start.9 = (bf16[1024,512]{1,0:T(8,128)(2,1)S(1)}, bf16[1024,512]{1,0:T(8,128)(2,1)S(1)}, u32[]{:S(2)}, u32[]{:S(2)}) collective-permute-start(bf16[1024,512]{1,0:T(8,128)(2,1)S(1)} %collective-permute-done.8), channel_id=1, source_target_pairs={{448,0},{456,8},{464,16},{472,24},{480,32},{488,40},{496,48},{504,... | collective-permute-start | bytes 3145736 | tf_op jit(solution)/shard_map/ppermute | solution.py:12
  249.1 24.8 %collective-permute-start.10 = (bf16[1024,512]{1,0:T(8,128)(2,1)S(1)}, bf16[1024,512]{1,0:T(8,128)(2,1)S(1)}, u32[]{:S(2)}, u32[]{:S(2)}) collective-permute-start(bf16[1024,512]{1,0:T(8,128)(2,1)S(1)} %collective-permute-done.9), channel_id=1, source_target_pairs={{448,0},{456,8},{464,16},{472,24},{480,32},{488,40},{496,48},{504,... | collective-permute-start | bytes 3145736 | tf_op jit(solution)/shard_map/ppermute | solution.py:12
  273.9 1.9 copy-start.5
  273.9 23.9 %collective-permute-start.11 = (bf16[1024,512]{1,0:T(8,128)(2,1)S(1)}, bf16[1024,512]{1,0:T(8,128)(2,1)}, u32[]{:S(2)}, u32[]{:S(2)}) collective-permute-start(bf16[1024,512]{1,0:T(8,128)(2,1)S(1)} %collective-permute-done.10), channel_id=1, source_target_pairs={{448,0},{456,8},{464,16},{472,24},{480,32},{488,40},{496,48},{504,... | collective-permute-start | bytes 3145736 | tf_op jit(solution)/shard_map/ppermute | solution.py:12
  297.7 23.5 %collective-permute-start.12 = (bf16[1024,512]{1,0:T(8,128)(2,1)}, bf16[1024,512]{1,0:T(8,128)(2,1)}, u32[]{:S(2)}, u32[]{:S(2)}) collective-permute-start(bf16[1024,512]{1,0:T(8,128)(2,1)} %collective-permute-done.11), channel_id=1, source_target_pairs={{448,0},{456,8},{464,16},{472,24},{480,32},{488,40},{496,48},{504,... | collective-permute-start | bytes 3145736 | tf_op jit(solution)/shard_map/ppermute | solution.py:12
  300.4 46.0 %copy-start.8 = (s32[48]{0:T(128)S(1)}, s32[48]{0:T(128)}, u32[]{:S(2)}) copy-start(s32[48]{0:T(128)} %param.11) | copy-start | bytes 580
  321.2 22.3 %collective-permute-start.13 = (bf16[1024,512]{1,0:T(8,128)(2,1)}, bf16[1024,512]{1,0:T(8,128)(2,1)S(1)}, u32[]{:S(2)}, u32[]{:S(2)}) collective-permute-start(bf16[1024,512]{1,0:T(8,128)(2,1)} %collective-permute-done.12), channel_id=1, source_target_pairs={{448,0},{456,8},{464,16},{472,24},{480,32},{488,40},{496,48},{504,... | collective-permute-start | bytes 3145736 | tf_op jit(solution)/shard_map/ppermute | solution.py:12
  346.4 220.2 %copy-start.6 = (bf16[128,512]{1,0:T(8,128)(2,1)S(1)}, bf16[128,512]{1,0:T(8,128)(2,1)}, u32[]{:S(2)}) copy-start(bf16[128,512]{1,0:T(8,128)(2,1)} %param.15) | copy-start | bytes 393220
  361.5 669.5 %all-reduce.2.cloned.1.call-start = ((), (), s32[]{:S(2)}) async-start(), calls=%async_computation.2 | async-start | bytes 2097152 | tf_op jit(solution)/shard_map/psum | solution.py:70
Sparse Core Ops, SparseCore 0:
  361.6 203.0 reduce-scatter.1
  571.7 459.2 all-reduce.1
where the time goes:
time: 1040 us
  waiting for transfers between devices  951 us (91%)
  starting transfers between devices  31.9 us (3%)
  local copies, waits for them, and re-layouts  27.5 us (3%)
  between operations  14.9 us (1%)
    psum x1, waiting for transfers between devices, shards(): weight_grad = lax.psum(local_grad, ('dom', 'rep'))  462 us
    ppermute x14, waiting for transfers between devices, from_behind(): return lax.ppermute(block, axis, route)  286 us
    reduce_scatter x1, waiting for transfers between devices, shards(): lax.psum_scatter(partial_rows, 'rep', scatter_dimension=0, tiled=True)  203 us
    ppermute x14, starting transfers between devices, from_behind(): return lax.ppermute(block, axis, route)  31.8 us
  transfers between devices with their start and end apart: 16, of which 16 were waited for; matrix products, arithmetic and copies ran while one was open for 1% of the time, Pallas kernels for 0%

commit v1 on v0

v1 whole, which is shorter than its diff:
```python
import functools

import jax
import jax.numpy as jnp
from jax import lax
from jax.experimental import pallas as pl
from jax.experimental.pallas import tpu as pltpu
from jax.sharding import PartitionSpec as P

MESH = pl.DeviceIdType.MESH
BF16 = jnp.bfloat16
F32 = jnp.float32


def at(x, y, zl, zh, core):
    return zl * 8 + x * 2 + core, zh * 4 + y


def hosted(x, y, zh, core):
    c = (2 * x + core + 16 - 4 * zh - y) % 8
    natural, natural_core = c // 2, c % 2
    b = (x + 8 - natural - 2 * zh) % 4
    host_x = (x + b + 3) % 4
    side = ((host_x + 4 - natural) % 4 - 1) // 2
    host_y = natural_core * (1 - side) + (1 - natural_core) * (2 + side)
    return host_x, host_y


def class_of(host_y):
    natural_core = 1 - host_y // 2
    side = natural_core * (1 - host_y) + (1 - natural_core) * (host_y - 2)
    return side, natural_core


def set_of(host_x, host_y, zh, core):
    side, natural_core = class_of(host_y)
    moved = (side + zh) % 2
    right = 1 - natural_core * (1 - core) * 2
    x = (host_x + 4 + moved * right) % 4
    low = (1 - natural_core) * core + natural_core * (1 - core) * 3
    high = (1 - natural_core) * (2 + core) + natural_core * (1 + core)
    return x, moved * low + (1 - moved) * high


def place():
    dom, rep = lax.axis_index("dom"), lax.axis_index("rep")
    return (dom // 2) % 4, rep % 4, dom // 8, rep // 4, dom % 2


def z_neighbour(x, y, zl, zh, core, distance):
    z = (zh * 8 + zl + distance + 16) % 16
    return at(x, y, z % 8, z // 8, core)


def signal(device):
    pl.semaphore_signal(pltpu.get_barrier_semaphore(), inc=1, device_id=device, device_id_type=MESH)


UNITS = 2


def gather_kernel(features, blocks, own_send, own_recv, up_send, up_recv, down_send, down_recv, pair_send, pair_recv):
    x, y, zl, zh, core = place()
    side, natural_core = class_of(y)
    up = z_neighbour(x, y, zl, zh, core, 1)
    down = z_neighbour(x, y, zl, zh, core, -1)
    sibling = at(x, y, zl, zh, 1 - core)
    source = at((x + 3 + 2 * side) % 4, y, zl, zh, natural_core)
    target_x = (x + 1 + 2 * side) % 4
    half = features.shape[0] // 2
    unit = half // UNITS

    for device in (up, down, sibling, source):
        signal(device)

    @pl.when(core == natural_core)
    def _():
        pl.semaphore_wait(pltpu.get_barrier_semaphore(), 5)

    @pl.when(core != natural_core)
    def _():
        pl.semaphore_wait(pltpu.get_barrier_semaphore(), 3)

    def rows(h, of_core):
        return pl.ds(pl.multiple_of(of_core * half + h * unit, unit), unit)

    def part(distance, h, of_core):
        return blocks.at[(zl + distance + 8) % 8, rows(h, of_core)]

    def own_copy(h, to_core):
        return pltpu.make_async_remote_copy(
            src_ref=features.at[rows(h, to_core)],
            dst_ref=part(0, h, to_core),
            send_sem=own_send.at[h, to_core],
            recv_sem=own_recv.at[h],
            device_id=at(target_x, y, zl, zh, to_core),
            device_id_type=MESH,
        )

    @pl.when(core == natural_core)
    def _():
        for h in range(UNITS):
            for to_core in range(2):
                own_copy(h, to_core).start()

    def hop(step, h, upward):
        ref = part(-step if upward else step, h, core)
        send, recv = (up_send, up_recv) if upward else (down_send, down_recv)
        return pltpu.make_async_remote_copy(
            src_ref=ref,
            dst_ref=ref,
            send_sem=send.at[step, h],
            recv_sem=recv.at[step, h],
            device_id=up if upward else down,
            device_id_type=MESH,
        )

    def arrival(step, h, upward):
        ref = part(-step - 1 if upward else step + 1, h, core)
        send, recv = (up_send, up_recv) if upward else (down_send, down_recv)
        return pltpu.make_async_remote_copy(
            src_ref=ref,
            dst_ref=ref,
            send_sem=send.at[step, h],
            recv_sem=recv.at[step, h],
            device_id=up if upward else down,
            device_id_type=MESH,
        )

    def to_sibling(distance, h):
        ref = part(distance, h, core)
        return pltpu.make_async_remote_copy(
            src_ref=ref,
            dst_ref=ref,
            send_sem=pair_send.at[distance + 4, h],
            recv_sem=pair_recv.at[distance + 4, h],
            device_id=sibling,
            device_id_type=MESH,
        )

    def from_sibling(distance, h):
        ref = part(distance, h, 1 - core)
        return pltpu.make_async_remote_copy(
            src_ref=ref,
            dst_ref=ref,
            send_sem=pair_send.at[distance + 4, h],
            recv_sem=pair_recv.at[distance + 4, h],
            device_id=sibling,
            device_id_type=MESH,
        )

    def last(h, upward):
        return 4 if (h < UNITS // 2) == upward else 3

    for h in range(UNITS):
        own_copy(h, 0).wait_recv()
        hop(0, h, True).start()
        hop(0, h, False).start()
        to_sibling(0, h).start()
    for step in range(4):
        for h in range(UNITS):
            for upward in (True, False):
                if step < last(h, upward):
                    arrival(step, h, upward).wait_recv()
                    if step + 1 < last(h, upward):
                        hop(step + 1, h, upward).start()
                    distance = -step - 1 if upward else step + 1
                    if distance == 4:
                        distance = -4
                    to_sibling(distance, h).start()
    for distance in range(-4, 4):
        for h in range(UNITS):
            from_sibling(distance, h).wait_recv()
    for distance in range(-4, 4):
        for h in range(UNITS):
            to_sibling(distance, h).wait_send()
    for step in range(4):
        for h in range(UNITS):
            for upward in (True, False):
                if step < last(h, upward):
                    hop(step, h, upward).wait_send()

    @pl.when(core == natural_core)
    def _():
        for h in range(UNITS):
            for to_core in range(2):
                own_copy(h, to_core).wait_send()


def gather(features):
    nodes, width = features.shape
    sems = pltpu.SemaphoreType.DMA
    return pl.pallas_call(
        gather_kernel,
        out_shape=jax.ShapeDtypeStruct((8, nodes, width), features.dtype),
        in_specs=[pl.BlockSpec(memory_space=pl.ANY)],
        out_specs=pl.BlockSpec(memory_space=pl.ANY),
        scratch_shapes=[
            sems((UNITS, 2)),
            sems((UNITS,)),
            sems((4, UNITS)),
            sems((4, UNITS)),
            sems((4, UNITS)),
            sems((4, UNITS)),
            sems((8, UNITS)),
            sems((8, UNITS)),
        ],
        compiler_params=pltpu.CompilerParams(collective_id=0, has_side_effects=True),
        name="gather",
    )(features)


def tile_kernel(rows, cols, count, tiles, blocks, out, total):
    total[...] = jnp.zeros_like(total)

    def one(slot, carry):
        col = cols[slot]
        block = blocks[(col // 64) * 8 + col % 8]
        total[rows[slot]] += jnp.dot(tiles[slot], block, preferred_element_type=F32)
        return carry

    lax.fori_loop(0, count[0], one, 0)
    out[...] = total[...].astype(out.dtype)


def tile_products(rows, cols, count, tiles, blocks):
    width = blocks.shape[-1]
    smem = pl.BlockSpec(memory_space=pltpu.SMEM)
    vmem = pl.BlockSpec(memory_space=pltpu.VMEM)
    return pl.pallas_call(
        tile_kernel,
        out_shape=jax.ShapeDtypeStruct((8, 128, width), BF16),
        in_specs=[smem, smem, smem, vmem, vmem],
        out_specs=vmem,
        scratch_shapes=[pltpu.VMEM((8, 128, width), F32)],
        compiler_params=pltpu.CompilerParams(vmem_limit_bytes=40 * 2**20),
        name="tile_products",
    )(rows, cols, count, tiles, blocks)


def finish_kernel(
    partial, weight, cotangent, node_out, weight_grad,
    plane_in, z_in, z_out, agg, slope, grad, grad_in, piece, piece_in, total, total_in, whole,
    plane_send, plane_recv, z_sems, agg_sems, slope_sems, grad_send, grad_recv,
    piece_send, piece_recv, total_send, total_recv, whole_send, whole_recv, last_sems,
):
    x, y, zl, zh, core = place()
    z = zh * 8 + zl
    spot = x * 4 + y
    sibling = at(x, y, zl, zh, 1 - core)

    def in_plane(distance):
        there = (spot + distance) % 16
        return at(there // 4, there % 4, zl, zh, core)

    for distance in range(1, 16):
        signal(in_plane(distance))
    for distance in range(1, 16):
        signal(z_neighbour(x, y, zl, zh, core, distance))
    signal(sibling)
    pl.semaphore_wait(pltpu.get_barrier_semaphore(), 31)

    def remote(src, dst, send, recv, device):
        return pltpu.make_async_remote_copy(
            src_ref=src, dst_ref=dst, send_sem=send, recv_sem=recv, device_id=device, device_id_type=MESH
        )

    set_x, set_y = set_of(x, y, zh, core)
    here = (set_x + 4 - x) % 4 == 0

    def to_owner(distance):
        there = (y + distance) % 4
        return remote(
            partial.at[:, there], plane_in.at[set_y], plane_send.at[distance], plane_recv.at[set_y],
            at(set_x, there, zl, zh, core),
        )

    def to_self():
        return pltpu.make_async_copy(partial.at[:, y], plane_in.at[set_y], plane_recv.at[set_y])

    for distance in (2, 1, 3):
        to_owner(distance).start()

    @pl.when(here)
    def _():
        to_self().start()

    @pl.when(jnp.logical_not(here))
    def _():
        to_owner(0).start()

    for member in range(4):
        remote(plane_in.at[member], plane_in.at[member], plane_send.at[0], plane_recv.at[member], sibling).wait_recv()

    def summed(part):
        result = plane_in[0, part].astype(F32)
        for member in range(1, 4):
            result += plane_in[member, part].astype(F32)
        return result

    z_out[...] = summed(1 - zh).astype(BF16)
    across = remote(z_out, z_in, z_sems.at[0], z_sems.at[1], z_neighbour(x, y, zl, zh, core, 8))
    across.start()
    own = summed(zh)
    across.wait_recv()
    mine = (own + z_in[...].astype(F32)).astype(BF16)
    agg[core] = mine
    agg_copy = remote(agg.at[core], agg.at[core], agg_sems.at[0], agg_sems.at[1], sibling)
    agg_copy.start()

    pre = jnp.dot(mine, weight[...], preferred_element_type=F32)
    sigma = jax.nn.sigmoid(pre)
    node_out[...] = (pre * sigma).astype(node_out.dtype)
    slope[core] = (cotangent[...].astype(F32) * sigma * (1.0 + pre * (1.0 - sigma))).astype(BF16)
    slope_copy = remote(slope.at[core], slope.at[core], slope_sems.at[0], slope_sems.at[1], sibling)
    slope_copy.start()
    agg_copy.wait_recv()
    slope_copy.wait_recv()

    columns = pl.ds(pl.multiple_of(core * 256, 256), 256)
    local = lax.dot_general(
        agg[:, :, columns].reshape(256, 256), slope[...].reshape(256, 512),
        (((0,), (0,)), ((), ())), preferred_element_type=F32,
    )
    grad[...] = local.reshape(16, 16, 512).astype(BF16)

    def grad_copy(distance):
        there = (spot + distance) % 16
        return remote(
            grad.at[there], grad_in.at[spot], grad_send.at[distance], grad_recv.at[spot], in_plane(distance)
        )

    for distance in range(1, 16):
        grad_copy(distance).start()
    rows_sum = grad[spot].astype(F32)
    for distance in range(1, 16):
        there = (spot + distance) % 16
        remote(grad_in.at[there], grad_in.at[there], grad_send.at[0], grad_recv.at[there], sibling).wait_recv()
        rows_sum += grad_in[there].astype(F32)
    for j in range(8):
        piece[j] = rows_sum[8 * (j // 4) : 8 * (j // 4) + 8, 128 * (j % 4) : 128 * (j % 4) + 128]

    def piece_copy(distance):
        there = (z + distance) % 16
        return remote(
            piece.at[there % 8], piece_in.at[z], piece_send.at[distance], piece_recv.at[z],
            z_neighbour(x, y, zl, zh, core, distance),
        )

    order = (8, 7, 9, 6, 10, 5, 11, 4, 12, 3, 13, 2, 14, 1, 15)
    for distance in order:
        piece_copy(distance).start()
    piece_in[z] = piece[zl]
    for distance in range(1, 16):
        there = (z + distance) % 16
        remote(piece_in.at[there], piece_in.at[there], piece_send.at[0], piece_recv.at[there], sibling).wait_recv()
    result = piece_in[0]
    for j in range(1, 16):
        result += piece_in[j]
    total[...] = result
    total_in[zl] = result

    def total_copy(distance):
        return remote(
            total, total_in.at[zl], total_send.at[distance + 3], total_recv.at[zl],
            z_neighbour(x, y, zl, zh, core, distance),
        )

    near = (4, -3, 3, -2, 2, -1, 1)
    for distance in near:
        total_copy(distance).start()
    for distance in range(1, 8):
        there = (zl + distance) % 8
        remote(total, total_in.at[there], total_send.at[0], total_recv.at[there], sibling).wait_recv()
    upper = jnp.concatenate([total_in[j] for j in range(4)], axis=1)
    lower = jnp.concatenate([total_in[j] for j in range(4, 8)], axis=1)
    whole[core, spot] = jnp.concatenate([upper, lower], axis=0).astype(BF16)

    def whole_copy(distance):
        return remote(
            whole.at[core, spot], whole.at[core, spot], whole_send.at[distance], whole_recv.at[spot],
            in_plane(distance),
        )

    for distance in range(1, 16):
        whole_copy(distance).start()
    for distance in range(1, 16):
        there = (spot + distance) % 16
        remote(
            whole.at[core, there], whole.at[core, there], whole_send.at[0], whole_recv.at[there], sibling
        ).wait_recv()
    final = remote(whole.at[core], whole.at[core], last_sems.at[0], last_sems.at[1], sibling)
    final.start()
    final.wait_recv()
    weight_grad[...] = whole[...].reshape(512, 512).astype(F32)

    for distance in (1, 2, 3):
        to_owner(distance).wait_send()

    @pl.when(jnp.logical_not(here))
    def _():
        to_owner(0).wait_send()

    across.wait_send()
    agg_copy.wait_send()
    slope_copy.wait_send()
    for distance in range(1, 16):
        grad_copy(distance).wait_send()
        piece_copy(distance).wait_send()
        whole_copy(distance).wait_send()
    for distance in near:
        total_copy(distance).wait_send()
    final.wait_send()


def finish(partial, weight, cotangent):
    sems = pltpu.SemaphoreType.DMA
    vmem = pl.BlockSpec(memory_space=pltpu.VMEM)
    return pl.pallas_call(
        finish_kernel,
        out_shape=(
            jax.ShapeDtypeStruct(cotangent.shape, BF16),
            jax.ShapeDtypeStruct(weight.shape, F32),
        ),
        in_specs=[vmem] * 3,
        out_specs=(vmem, vmem),
        scratch_shapes=[
            pltpu.VMEM((4, 2, 128, 512), BF16),
            pltpu.VMEM((128, 512), BF16),
            pltpu.VMEM((128, 512), BF16),
            pltpu.VMEM((2, 128, 512), BF16),
            pltpu.VMEM((2, 128, 512), BF16),
            pltpu.VMEM((16, 16, 512), BF16),
            pltpu.VMEM((16, 16, 512), BF16),
            pltpu.VMEM((8, 8, 128), F32),
            pltpu.VMEM((16, 8, 128), F32),
            pltpu.VMEM((8, 128), F32),
            pltpu.VMEM((8, 8, 128), F32),
            pltpu.VMEM((2, 16, 16, 512), BF16),
            sems((4,)),
            sems((4,)),
            sems((2,)),
            sems((2,)),
            sems((2,)),
            sems((16,)),
            sems((16,)),
            sems((16,)),
            sems((16,)),
            sems((8,)),
            sems((8,)),
            sems((16,)),
            sems((16,)),
            sems((2,)),
        ],
        compiler_params=pltpu.CompilerParams(
            collective_id=1, has_side_effects=True, vmem_limit_bytes=40 * 2**20
        ),
        name="finish",
    )(partial, weight, cotangent)


def tile_moves():
    moves = []
    for device in range(512):
        dom, rep = device // 8, device % 8
        x, y, zl, zh, core = (dom // 2) % 4, rep % 4, dom // 8, rep // 4, dom % 2
        host_x, host_y = hosted(x, y, zh, core)
        host = at(host_x, host_y, zl, zh, core)
        moves.append((device, host[0] * 8 + host[1]))
    return moves


def shards(features, tiles, tile_rows, tile_cols, tile_count, weight, cotangent):
    moves = tile_moves()
    axes = ("dom", "rep")
    slots = tile_rows.shape[0]
    numbers = lax.ppermute(jnp.concatenate([tile_rows, tile_cols, tile_count]), axes, moves)
    moved = lax.ppermute(tiles, axes, moves)
    blocks = gather(features)
    partial = tile_products(
        numbers[:slots], numbers[slots : 2 * slots], numbers[2 * slots :], moved, blocks.reshape(64, 128, 512)
    )
    return finish(partial.reshape(2, 4, 128, 512), weight, cotangent)


def solution(mesh):
    in_specs = (
        P("dom", None),
        P(("dom", "rep"), None, None),
        P(("dom", "rep")),
        P(("dom", "rep")),
        P(("dom", "rep")),
        P(),
        P(("dom", "rep"), None),
    )
    out_specs = (P(("dom", "rep"), None), P())
    return jax.shard_map(shards, mesh=mesh, in_specs=in_specs, out_specs=out_specs, check_vma=False)
```

time: 1040 us -> 185 us (0.18)
  waiting for transfers between devices: 951 us -> 0.01 us
  Pallas kernels: 0 us -> 169 us
  starting transfers between devices: 31.9 us -> 7.66 us
  local copies, waits for them, and re-layouts: 27.5 us -> 5.67 us
  between operations: 14.9 us -> 1.34 us
    psum x1 -> x0, waiting for transfers between devices: 462 us -> none  [shards(): weight_grad = lax.psum(local_grad, ('dom', 'rep'))]
    ppermute x14 -> x2, waiting for transfers between devices: 286 us -> 0.01 us  [the longest x1 0.01 us: shards(): lax.ppermute(jnp.concatenate([tile_rows, tile_cols, tile_count]), axes, m...]
    reduce_scatter x1 -> x0, waiting for transfers between devices: 203 us -> none  [shards(): lax.psum_scatter(partial_rows, 'rep', scatter_dimension=0, tiled=True)]
    pallas_call x0 -> x3, Pallas kernels: none -> 169 us  [the longest x1 87.1 us: gather(): pl.pallas_call(gather_kernel, out_shape=jax.ShapeDtypeStruct((8, nodes, w...]
    ppermute x14 -> x2, starting transfers between devices: 31.8 us -> 7.66 us  [the longest x1 5.22 us: shards(): moved = lax.ppermute(tiles, axes, moves)]
    unnamed x25 -> x8, local copies, waits for them, and re-layouts: 16.4 us -> 5.02 us
  transfers between devices with their start and end apart: 16 -> 2, of which waited for: 16 -> 0; matrix products, arithmetic and copies ran while one was open for 1% -> 1% of each run, Pallas kernels for 0% -> 47%
where the time goes in v1:
time: 185 us
  Pallas kernels  169 us (91%)
  starting transfers between devices  7.66 us (4%)
  local copies, waits for them, and re-layouts  5.67 us (3%)
    pallas_call x1, Pallas kernels, gather(): pl.pallas_call(gather_kernel, out_shape=jax.ShapeDtypeStruct((8, nodes, w...  87.1 us
    pallas_call x1, Pallas kernels, finish(): pl.pallas_call(finish_kernel, out_shape=(jax.ShapeDtypeStruct(cotangent.s...  77.2 us
    ppermute x1, starting transfers between devices, shards(): moved = lax.ppermute(tiles, axes, moves)  5.22 us
    unnamed x8, local copies, waits for them, and re-layouts  5.02 us
    pallas_call x1, Pallas kernels, tile_products(): pl.pallas_call(tile_kernel, out_shape=jax.ShapeDtypeStruct((8, 128, width...  4.85 us
  transfers between devices with their start and end apart: 2, of which 0 were waited for; matrix products, arithmetic and copies ran while one was open for 1% of the time, Pallas kernels for 47%

profile of v1, /device:TPU:1, one launch (start us, length us, event | category | flops | bytes accessed | tf_op | source)
XLA Modules:
  0.0 184.7 jit_solution(4384389001353132817)
XLA Ops:
  0.6 5.2 %collective-permute-start.1 = (bf16[48,128,128]{2,1,0:T(8,128)(2,1)}, bf16[48,128,128]{2,1,0:T(8,128)(2,1)S(1)}, u32[]{:S(2)}, u32[]{:S(2)}) collective-permute-start(bf16[48,128,128]{2,1,0:T(8,128)(2,1)} %param.8), channel_id=1, source_target_pairs={{0,51},{1,1},{2,2},{3,16},{4,54},{5,4},{6,7},{7,21},{8,56},{9,59},... | collective-permute-start | bytes 4718600 | tf_op jit(solution)/shard_map/ppermute | solution.py:478
  6.5 0.7 pad_add_fusion
  7.2 2.4 %collective-permute-start = (s32[97]{0:T(128)S(1)}, s32[97]{0:T(128)S(1)}, u32[]{:S(2)}, u32[]{:S(2)}) collective-permute-start(s32[97]{0:T(128)S(1)} %pad_add_fusion), channel_id=1, source_target_pairs={{0,51},{1,1},{2,2},{3,16},{4,54},{5,4},{6,7},{7,21},{8,56},{9,59},... | collective-permute-start | bytes 1172 | tf_op jit(solution)/shard_map/ppermute | solution.py:477
  9.7 87.1 %gather.1 = bf16[8,1024,512]{2,1,0:T(8,128)(2,1)} custom-call(bf16[1024,512]{1,0:T(8,128)(2,1)} %features.1), custom_call_target="tpu_custom_call" | custom-call | tf_op jit(solution)/shard_map/gather/pallas_call | solution.py:193
  96.9 0.0 collective-permute-done
  96.9 0.6 slice.11.count
  97.4 0.1 fusion
  97.5 0.0 collective-permute-done.1.tiles
  97.5 0.0 copy-start
  97.5 3.4 %copy-done = bf16[8,1024,512]{2,1,0:T(8,128)(2,1)S(1)} copy-done((bf16[8,1024,512]{2,1,0:T(8,128)(2,1)S(1)}, bf16[8,1024,512]{2,1,0:T(8,128)(2,1)}, u32[]{:S(2)}) %copy-start) | copy-done | bytes 8388632
  100.9 0.0 copy-start.1
  100.9 0.0 copy-start.2
  100.9 4.9 %tile_products.1 = bf16[8,128,512]{2,1,0:T(8,128)(2,1)S(1)} custom-call(s32[48]{0:T(128)S(1)} %get-tuple-element.3.rows, s32[48]{0:T(128)S(1)} %get-tuple-element.2.cols, s32[1]{0:T(128)} %slice.11.count, bf16[48,128,128]{2,1,0:T(8,128)(2,1)S(1)} %collective-permute-done.1.tiles, bf16[64,128,512]{2,1,0:T(8,128)(2,1)S(1)} %bitcast.2), custom_call_target="tpu_custom_call" | custom-call | tf_op jit(solution)/shard_map/tile_products/pallas_call | solution.py:230
  105.8 0.0 copy-done.1
  105.8 0.0 copy-done.2
  105.8 77.2 %finish.1 = (bf16[128,512]{1,0:T(8,128)(2,1)S(1)}, f32[512,512]{1,0:T(8,128)S(1)}) custom-call(bf16[2,4,128,512]{3,2,1,0:T(8,128)(2,1)S(1)} %bitcast.3, bf16[512,512]{1,0:T(8,128)(2,1)S(1)} %copy-done.1, bf16[128,512]{1,0:T(8,128)(2,1)S(1)} %copy-done.2), custom_call_target="tpu_custom_call" | custom-call | tf_op jit(solution)/shard_map/finish/pallas_call | solution.py:419
  183.1 0.7 copy.12
  183.7 1.0 copy.13
Async XLA Ops:
  0.6 96.9 %collective-permute-start.1 = (bf16[48,128,128]{2,1,0:T(8,128)(2,1)}, bf16[48,128,128]{2,1,0:T(8,128)(2,1)S(1)}, u32[]{:S(2)}, u32[]{:S(2)}) collective-permute-start(bf16[48,128,128]{2,1,0:T(8,128)(2,1)} %param.8), channel_id=1, source_target_pairs={{0,51},{1,1},{2,2},{3,16},{4,54},{5,4},{6,7},{7,21},{8,56},{9,59},... | collective-permute-start | bytes 4718600 | tf_op jit(solution)/shard_map/ppermute | solution.py:478
  7.2 89.6 %collective-permute-start = (s32[97]{0:T(128)S(1)}, s32[97]{0:T(128)S(1)}, u32[]{:S(2)}, u32[]{:S(2)}) collective-permute-start(s32[97]{0:T(128)S(1)} %pad_add_fusion), channel_id=1, source_target_pairs={{0,51},{1,1},{2,2},{3,16},{4,54},{5,4},{6,7},{7,21},{8,56},{9,59},... | collective-permute-start | bytes 1172 | tf_op jit(solution)/shard_map/ppermute | solution.py:477
  97.5 3.4 %copy-start = (bf16[8,1024,512]{2,1,0:T(8,128)(2,1)S(1)}, bf16[8,1024,512]{2,1,0:T(8,128)(2,1)}, u32[]{:S(2)}) copy-start(bf16[8,1024,512]{2,1,0:T(8,128)(2,1)} %gather.1) | copy-start | bytes 25165828
  100.9 4.9 %copy-start.1 = (bf16[512,512]{1,0:T(8,128)(2,1)S(1)}, bf16[512,512]{1,0:T(8,128)(2,1)}, u32[]{:S(2)}) copy-start(bf16[512,512]{1,0:T(8,128)(2,1)} %weight.1) | copy-start | bytes 1572868
  100.9 4.9 %copy-start.2 = (bf16[128,512]{1,0:T(8,128)(2,1)S(1)}, bf16[128,512]{1,0:T(8,128)(2,1)}, u32[]{:S(2)}) copy-start(bf16[128,512]{1,0:T(8,128)(2,1)} %cotangent.1) | copy-start | bytes 393220

commit v2 on v0

v2 whole, which is shorter than its diff:
```python
import types

import jax
import jax.numpy as jnp
from jax import lax
from jax.experimental import pallas as pl
from jax.experimental.pallas import tpu as pltpu
from jax.sharding import PartitionSpec as P

MESH = pl.DeviceIdType.MESH
BF16 = jnp.bfloat16
F32 = jnp.float32
I32 = jnp.int32

WIDTHS = (256, 128, 128)
UNITS = 2
SLOTS = 48
SLOT_STEP = 6


def at(x, y, zl, zh, core):
    return zl * 8 + x * 2 + core, zh * 4 + y


def hosted(x, y, zh, core):
    c = (2 * x + core + 16 - 4 * zh - y) % 8
    natural, natural_core = c // 2, c % 2
    b = (x + 8 - natural - 2 * zh) % 4
    host_x = (x + b + 3) % 4
    side = ((host_x + 4 - natural) % 4 - 1) // 2
    host_y = (1 - side) * (1 - natural_core) + side * (2 + natural_core)
    return host_x, host_y


def class_of(host_y):
    return host_y // 2, ((host_y + 1) // 2 + 1) % 2


def set_of(host_x, host_y, zh, core):
    side, natural_core = class_of(host_y)
    moved = (side + zh) % 2
    right = 1 - natural_core * (1 - core) * 2
    x = (host_x + 4 + moved * right) % 4
    low = (1 - natural_core) * core + natural_core * (1 - core) * 3
    high = (1 - natural_core) * (2 + core) + natural_core * (1 + core)
    return x, moved * low + (1 - moved) * high


def place():
    dom, rep = lax.axis_index("dom"), lax.axis_index("rep")
    return (dom // 2) % 4, rep % 4, dom // 8, rep // 4, dom % 2


def z_neighbour(x, y, zl, zh, core, distance):
    z = (zh * 8 + zl + distance + 16) % 16
    return at(x, y, z % 8, z // 8, core)


def signal(device):
    pl.semaphore_signal(pltpu.get_barrier_semaphore(), inc=1, device_id=device, device_id_type=MESH)


def remote(src, dst, send, recv, device):
    return pltpu.make_async_remote_copy(
        src_ref=src, dst_ref=dst, send_sem=send, recv_sem=recv, device_id=device, device_id_type=MESH
    )


def when_not(condition, action):
    pl.when(jnp.logical_not(condition))(action)


def sort_slots(rows, cols, count, numbers):
    shape = (SLOTS, SLOTS)
    sub = lax.broadcasted_iota(I32, shape, 0).astype(F32)
    lane = lax.broadcasted_iota(I32, shape, 1).astype(F32)
    eye = (sub == lane).astype(F32)

    def column(row):
        return jnp.sum(eye * row, axis=1, keepdims=True)

    live = lane[:1] < count[...].reshape(1, 1).astype(F32)
    key = jnp.where(live, rows[...].reshape(1, SLOTS).astype(F32), 8.0)
    col = cols[...].reshape(1, SLOTS)
    block = ((col >> 6) * 8 + (col & 7)).astype(F32)
    unique = key * 64.0 + lane[:1]
    key_column = column(key)
    rank = jnp.sum((unique < column(unique)).astype(F32), axis=1, keepdims=True)
    chosen = (rank == lane).astype(F32)
    after = (rank + 1.0 == lane).astype(F32)
    sorted_key = jnp.sum(chosen * key_column, axis=0, keepdims=True)
    key_before = jnp.sum(after * key_column, axis=0, keepdims=True)
    numbers[0:1, 0:SLOTS] = jnp.sum(chosen * sub, axis=0, keepdims=True).astype(I32)
    numbers[1:2, 0:SLOTS] = jnp.sum(chosen * column(block), axis=0, keepdims=True).astype(I32)
    numbers[2:3, 0:SLOTS] = (sorted_key == key_before).astype(I32)
    ends = jnp.where(key_column == lane, rank + 1.0, 0.0)
    numbers[3:4, 0:SLOTS] = jnp.max(ends, axis=0, keepdims=True).astype(I32)


def scratch():
    vmem, sems = pltpu.VMEM, pltpu.SemaphoreType.DMA
    chunks = len(WIDTHS)
    names = {
        "numbers": vmem((8, 128), I32),
        "numbers_in": vmem((8, 128), I32),
        "table": pltpu.SMEM((8, 128), I32),
        "tile_set": vmem((SLOTS, 128, 128), BF16),
        "products": vmem((SLOTS + 1, 128, max(WIDTHS)), F32),
        "weight": vmem((512, 512), BF16),
        "cotangent": vmem((128, 512), BF16),
        "load_sems": sems((2,)),
        "agg": vmem((2, 128, 512), BF16),
        "slope": vmem((2, 128, 512), BF16),
        "grad": vmem((16, 16, 512), BF16),
        "grad_in": vmem((16, 16, 512), BF16),
        "piece": vmem((8, 8, 128), F32),
        "piece_in": vmem((16, 8, 128), F32),
        "total": vmem((8, 128), F32),
        "total_in": vmem((8, 8, 128), F32),
        "whole": vmem((2, 16, 16, 512), BF16),
        "set_sems": sems((5,)),
        "own_send": sems((chunks, UNITS, 2)),
        "own_recv": sems((chunks, UNITS)),
        "ring_send": sems((chunks, 2, 4, UNITS)),
        "ring_recv": sems((chunks, 2, 4, UNITS)),
        "pair_send": sems((chunks, 8, UNITS)),
        "pair_recv": sems((chunks, 8, UNITS)),
        "plane_send": sems((chunks, 4)),
        "plane_recv": sems((chunks, 4)),
        "z_send": sems((chunks,)),
        "z_recv": sems((chunks,)),
        "agg_send": sems((chunks,)),
        "agg_recv": sems((chunks,)),
        "slope_sems": sems((2,)),
        "grad_send": sems((16,)),
        "grad_recv": sems((16,)),
        "piece_send": sems((16,)),
        "piece_recv": sems((16,)),
        "total_send": sems((8,)),
        "total_recv": sems((8,)),
        "whole_send": sems((16,)),
        "whole_recv": sems((16,)),
        "last_sems": sems((2,)),
    }
    for q, width in enumerate(WIDTHS):
        names["blocks%d" % q] = vmem((64, 128, width), BF16)
        names["partial%d" % q] = vmem((2, 4, 128, width), BF16)
        names["plane_in%d" % q] = vmem((4, 2, 128, width), BF16)
        names["z_out%d" % q] = vmem((128, width), BF16)
        names["z_in%d" % q] = vmem((128, width), BF16)
        names["own%d" % q] = vmem((128, width), F32)
    return names


def layer_kernel(features, tiles, rows, cols, count, weight_in, cotangent_in, node_out, weight_grad, *refs):
    s = types.SimpleNamespace(**dict(zip(scratch(), refs)))
    chunks = len(WIDTHS)
    starts = [sum(WIDTHS[:q]) for q in range(chunks)]

    def of(name, q):
        return getattr(s, name + str(q))

    x, y, zl, zh, core = place()
    z = zh * 8 + zl
    spot = x * 4 + y
    sibling = at(x, y, zl, zh, 1 - core)
    up = z_neighbour(x, y, zl, zh, core, 1)
    down = z_neighbour(x, y, zl, zh, core, -1)
    side, natural_core = class_of(y)
    is_source = core == natural_core
    source = at((x + 3 + 2 * side) % 4, y, zl, zh, natural_core)
    target_x = (x + 1 + 2 * side) % 4

    def in_plane(distance):
        there = (spot + distance) % 16
        return at(there // 4, there % 4, zl, zh, core)

    weight, cotangent = s.weight, s.cotangent
    loads = [
        pltpu.make_async_copy(weight_in, weight, s.load_sems.at[0]),
        pltpu.make_async_copy(cotangent_in, cotangent, s.load_sems.at[1]),
    ]
    for load in loads:
        load.start()

    signal(up)
    signal(down)
    signal(sibling)
    when_not(is_source, lambda: signal(source))
    for distance in (8, 7, 9, 6, 10, 5, 11, 4, 12, 3, 13, 2, 14):
        signal(z_neighbour(x, y, zl, zh, core, distance))
    for distance in range(1, 16):
        signal(in_plane(distance))
    sort_slots(rows, cols, count, s.numbers)
    s.products[0] = jnp.zeros(s.products.shape[1:], F32)
    pl.semaphore_wait(pltpu.get_barrier_semaphore(), 31 + (1 - (core + natural_core) % 2))

    def block_part(q, distance, h, of_core):
        size = 4 // UNITS
        return of("blocks", q).at[pl.ds((zl + distance + 8) % 8 * 8 + of_core * 4 + h * size, size)]

    def own_copy(q, h, to_core):
        size = 4 // UNITS
        return remote(
            features.at[pl.ds(to_core * 4 + h * size, size), :, pl.ds(starts[q], WIDTHS[q])],
            block_part(q, 0, h, to_core), s.own_send.at[q, h, to_core], s.own_recv.at[q, h],
            at(target_x, y, zl, zh, to_core),
        )

    def send_own(q):
        @pl.when(is_source)
        def _():
            for h in range(UNITS):
                for to_core in range(2):
                    own_copy(q, h, to_core).start()

    def hop(q, step, h, upward):
        ref = block_part(q, -step if upward else step, h, core)
        way = 0 if upward else 1
        return remote(
            ref, ref, s.ring_send.at[q, way, step, h], s.ring_recv.at[q, way, step, h], up if upward else down
        )

    def arrival(q, step, h, upward):
        ref = block_part(q, -step - 1 if upward else step + 1, h, core)
        way = 0 if upward else 1
        return remote(ref, ref, s.ring_send.at[q, way, step, h], s.ring_recv.at[q, way, step, h], sibling)

    def pair_copy(q, distance, h, of_core):
        ref = block_part(q, distance, h, of_core)
        return remote(ref, ref, s.pair_send.at[q, distance + 4, h], s.pair_recv.at[q, distance + 4, h], sibling)

    def hops(h, upward):
        return 4 if (h < UNITS // 2) == upward else 3

    def own_event(q, h):
        own_copy(q, h, 0).wait_recv()
        hop(q, 0, h, True).start()
        hop(q, 0, h, False).start()
        pair_copy(q, 0, h, core).start()

    def ring_event(q, step, h, upward):
        arrival(q, step, h, upward).wait_recv()
        if step + 1 < hops(h, upward):
            hop(q, step + 1, h, upward).start()
        distance = -step - 1 if upward or step == 3 else step + 1
        pair_copy(q, distance, h, core).start()

    def ring_events(q, steps):
        return [
            lambda step=step, h=h, upward=upward: ring_event(q, step, h, upward)
            for step in steps
            for h in range(UNITS)
            for upward in (True, False)
            if step < hops(h, upward)
        ]

    def own_events(q):
        return [lambda h=h: own_event(q, h) for h in range(UNITS)]

    def pair_arrivals(q):
        for distance in (0, -1, 1, -2, 2, -3, 3, -4):
            for h in range(UNITS):
                pair_copy(q, distance, h, 1 - core).wait_recv()

    host_x, host_y = hosted(x, y, zh, core)
    stays = (host_x + 4 - x) % 4 + (host_y + 4 - y) % 4 == 0
    host = at(host_x, host_y, zl, zh, core)
    set_copies = [
        remote(s.numbers, s.numbers_in, s.set_sems.at[0], s.set_sems.at[1], host),
        remote(tiles, s.tile_set, s.set_sems.at[2], s.set_sems.at[3], host),
    ]
    local_copies = [
        pltpu.make_async_copy(s.numbers, s.numbers_in, s.set_sems.at[1]),
        pltpu.make_async_copy(tiles, s.tile_set, s.set_sems.at[3]),
    ]

    def send_set():
        @pl.when(stays)
        def _():
            for copy in local_copies:
                copy.start()

        @pl.when(jnp.logical_not(stays))
        def _():
            for copy in set_copies:
                copy.start()

    def receive_set():
        for copy in set_copies:
            copy.wait_recv()
        to_table = pltpu.make_async_copy(s.numbers_in, s.table, s.set_sems.at[4])
        to_table.start()
        to_table.wait()

    def entry(row, place, top):
        return jnp.minimum(jnp.maximum(s.table[row, place], 0), top)

    def multiply(q, first):
        width = WIDTHS[q]

        def one(j, carry):
            tile = s.tile_set[entry(0, j, SLOTS - 1)]
            product = jnp.dot(tile, of("blocks", q)[entry(1, j, 63)], preferred_element_type=F32)
            same = s.table[2, j].astype(F32)
            s.products[j + 1, :, 0:width] = product + same * s.products[j, :, 0:width]
            return carry

        lax.fori_loop(first, first + SLOT_STEP, one, 0)

    def multiplies(q):
        return [lambda first=first: multiply(q, first) for first in range(0, SLOTS, SLOT_STEP)]

    set_x, set_y = set_of(x, y, zh, core)
    here = (set_x + 4 - x) % 4 == 0

    def to_owner(q, distance):
        there = (y + distance) % 4
        return remote(
            of("partial", q).at[:, there], of("plane_in", q).at[set_y], s.plane_send.at[q, distance],
            s.plane_recv.at[q, set_y], at(set_x, there, zl, zh, core),
        )

    def send_partial(q):
        width = WIDTHS[q]
        for t in range(8):
            of("partial", q)[t // 4, t % 4] = s.products[entry(3, t, SLOTS), :, 0:width].astype(BF16)
        for distance in (2, 1, 3):
            to_owner(q, distance).start()

        @pl.when(here)
        def _():
            pltpu.make_async_copy(
                of("partial", q).at[:, y], of("plane_in", q).at[set_y], s.plane_recv.at[q, set_y]
            ).start()

        when_not(here, lambda: to_owner(q, 0).start())

    def across(q):
        return remote(
            of("z_out", q), of("z_in", q), s.z_send.at[q], s.z_recv.at[q], z_neighbour(x, y, zl, zh, core, 8)
        )

    def sum_plane(q):
        for member in range(4):
            ref = of("plane_in", q).at[member]
            remote(ref, ref, s.plane_send.at[q, 0], s.plane_recv.at[q, member], sibling).wait_recv()

        def summed(part):
            result = of("plane_in", q)[0, part].astype(F32)
            for member in range(1, 4):
                result += of("plane_in", q)[member, part].astype(F32)
            return result

        of("z_out", q)[...] = summed(1 - zh).astype(BF16)
        across(q).start()
        of("own", q)[...] = summed(zh)

    def agg_copy(q, of_core):
        ref = s.agg.at[of_core, :, pl.ds(starts[q], WIDTHS[q])]
        return remote(ref, ref, s.agg_send.at[q], s.agg_recv.at[q], sibling)

    def aggregate(q):
        across(q).wait_recv()
        mine = (of("own", q)[...] + of("z_in", q)[...].astype(F32)).astype(BF16)
        s.agg[core, :, starts[q] : starts[q] + WIDTHS[q]] = mine
        agg_copy(q, core).start()
        return jnp.dot(mine, weight[starts[q] : starts[q] + WIDTHS[q], :], preferred_element_type=F32)

    events = []
    for slot in range(2 * chunks + 3):
        for q in range(chunks):
            step = slot - 2 * q - 1
            if step == -1:
                events += [(q, step, event) for event in own_events(q)]
            elif 0 <= step < 4:
                events += [(q, step, event) for event in ring_events(q, [step])]

    send_own(0)
    send_set()
    for q in range(1, chunks):
        send_own(q)
    work, waiting = [], list(range(chunks - 1))
    for place_in_list, (q, step, event) in enumerate(events):
        event()
        for _ in range(2):
            if work:
                work.pop(0)()
        left = [later[:2] for later in events[place_in_list + 1 :]]
        started = step >= 2 and q > 0 and (q, step) not in left
        if waiting and waiting[0] not in [later for later, _ in left] and (started or waiting[0] > 0):
            ready = waiting.pop(0)
            work.append(lambda ready=ready: pair_arrivals(ready))
            if ready == 0:
                work.append(receive_set)
            work += multiplies(ready) + [lambda ready=ready: send_partial(ready)]
    for item in work:
        item()
    for q in range(chunks - 2):
        sum_plane(q)
    pair_arrivals(chunks - 1)
    for item in multiplies(chunks - 1):
        item()
    send_partial(chunks - 1)
    sum_plane(chunks - 2)
    for load in loads:
        load.wait()
    pre = aggregate(0)
    for q in range(1, chunks - 1):
        pre += aggregate(q)
    sum_plane(chunks - 1)
    pre += aggregate(chunks - 1)

    sigma = jax.nn.sigmoid(pre)
    s.slope[core] = (cotangent[...].astype(F32) * sigma * (1.0 + pre * (1.0 - sigma))).astype(BF16)
    slope_copy = remote(s.slope.at[core], s.slope.at[core], s.slope_sems.at[0], s.slope_sems.at[1], sibling)
    slope_copy.start()
    node_out[...] = (pre * sigma).astype(node_out.dtype)
    for q in range(chunks):
        agg_copy(q, 1 - core).wait_recv()
    slope_copy.wait_recv()

    columns = pl.ds(pl.multiple_of(core * 256, 256), 256)
    local = lax.dot_general(
        s.agg[:, :, columns].reshape(256, 256), s.slope[...].reshape(256, 512),
        (((0,), (0,)), ((), ())), preferred_element_type=F32,
    )
    s.grad[...] = local.reshape(16, 16, 512).astype(BF16)

    def grad_copy(distance):
        there = (spot + distance) % 16
        return remote(
            s.grad.at[there], s.grad_in.at[spot], s.grad_send.at[distance], s.grad_recv.at[spot], in_plane(distance)
        )

    for distance in range(1, 16):
        grad_copy(distance).start()
    rows_sum = s.grad[spot].astype(F32)
    for distance in range(1, 16):
        there = (spot + distance) % 16
        ref = s.grad_in.at[there]
        remote(ref, ref, s.grad_send.at[0], s.grad_recv.at[there], sibling).wait_recv()
        rows_sum += s.grad_in[there].astype(F32)
    for j in range(8):
        s.piece[j] = rows_sum[8 * (j // 4) : 8 * (j // 4) + 8, 128 * (j % 4) : 128 * (j % 4) + 128]

    def piece_copy(distance):
        there = (z + distance) % 16
        return remote(
            s.piece.at[there % 8], s.piece_in.at[z], s.piece_send.at[distance], s.piece_recv.at[z],
            z_neighbour(x, y, zl, zh, core, distance),
        )

    for distance in (8, 7, 9, 6, 10, 5, 11, 4, 12, 3, 13, 2, 14, 1, 15):
        piece_copy(distance).start()
    s.piece_in[z] = s.piece[zl]
    for distance in range(1, 16):
        there = (z + distance) % 16
        ref = s.piece_in.at[there]
        remote(ref, ref, s.piece_send.at[0], s.piece_recv.at[there], sibling).wait_recv()
    result = s.piece_in[0]
    for j in range(1, 16):
        result += s.piece_in[j]
    s.total[...] = result
    s.total_in[zl] = result

    def total_copy(distance):
        return remote(
            s.total, s.total_in.at[zl], s.total_send.at[distance + 3], s.total_recv.at[zl],
            z_neighbour(x, y, zl, zh, core, distance),
        )

    near = (4, -3, 3, -2, 2, -1, 1)
    for distance in near:
        total_copy(distance).start()
    for distance in range(1, 8):
        there = (zl + distance) % 8
        remote(s.total, s.total_in.at[there], s.total_send.at[0], s.total_recv.at[there], sibling).wait_recv()
    upper = jnp.concatenate([s.total_in[j] for j in range(4)], axis=1)
    lower = jnp.concatenate([s.total_in[j] for j in range(4, 8)], axis=1)
    s.whole[core, spot] = jnp.concatenate([upper, lower], axis=0).astype(BF16)

    def whole_copy(distance):
        ref = s.whole.at[core, spot]
        return remote(ref, ref, s.whole_send.at[distance], s.whole_recv.at[spot], in_plane(distance))

    for distance in range(1, 16):
        whole_copy(distance).start()
    for distance in range(1, 16):
        there = (spot + distance) % 16
        ref = s.whole.at[core, there]
        remote(ref, ref, s.whole_send.at[0], s.whole_recv.at[there], sibling).wait_recv()
    final = remote(s.whole.at[core], s.whole.at[core], s.last_sems.at[0], s.last_sems.at[1], sibling)
    final.start()
    final.wait_recv()
    weight_grad[...] = s.whole[...].reshape(512, 512).astype(F32)

    for q in range(chunks):
        @pl.when(is_source)
        def _():
            for h in range(UNITS):
                for to_core in range(2):
                    own_copy(q, h, to_core).wait_send()

        for h in range(UNITS):
            for upward in (True, False):
                for step in range(hops(h, upward)):
                    hop(q, step, h, upward).wait_send()
            for distance in range(-4, 4):
                pair_copy(q, distance, h, core).wait_send()
        for distance in (1, 2, 3):
            to_owner(q, distance).wait_send()
        when_not(here, lambda: to_owner(q, 0).wait_send())
        across(q).wait_send()
        agg_copy(q, core).wait_send()

    @pl.when(jnp.logical_not(stays))
    def _():
        for copy in set_copies:
            copy.wait_send()

    slope_copy.wait_send()
    for distance in range(1, 16):
        grad_copy(distance).wait_send()
        piece_copy(distance).wait_send()
        whole_copy(distance).wait_send()
    for distance in near:
        total_copy(distance).wait_send()
    final.wait_send()


def shards(features, tiles, tile_rows, tile_cols, tile_count, weight, cotangent):
    vmem = pl.BlockSpec(memory_space=pltpu.VMEM)
    anywhere = pl.BlockSpec(memory_space=pl.ANY)
    return pl.pallas_call(
        layer_kernel,
        out_shape=(
            jax.ShapeDtypeStruct(cotangent.shape, BF16),
            jax.ShapeDtypeStruct(weight.shape, F32),
        ),
        in_specs=[anywhere, anywhere, vmem, vmem, vmem, anywhere, anywhere],
        out_specs=(vmem, vmem),
        scratch_shapes=list(scratch().values()),
        compiler_params=pltpu.CompilerParams(
            collective_id=0, has_side_effects=True, vmem_limit_bytes=60 * 2**20
        ),
        name="layer",
    )(
        features.reshape(8, 128, 512), tiles, tile_rows, tile_cols, tile_count, weight, cotangent,
    )


def solution(mesh):
    in_specs = (
        P("dom", None),
        P(("dom", "rep"), None, None),
        P(("dom", "rep")),
        P(("dom", "rep")),
        P(("dom", "rep")),
        P(),
        P(("dom", "rep"), None),
    )
    out_specs = (P(("dom", "rep"), None), P())
    return jax.shard_map(shards, mesh=mesh, in_specs=in_specs, out_specs=out_specs, check_vma=False)
```

time: 1040 us -> 140 us (0.13)
  waiting for transfers between devices: 951 us -> 0 us
  Pallas kernels: 0 us -> 135 us
  starting transfers between devices: 31.9 us -> 0 us
  local copies, waits for them, and re-layouts: 27.5 us -> 3.83 us
  between operations: 14.9 us -> 1.29 us
    psum x1 -> x0, waiting for transfers between devices: 462 us -> none  [shards(): weight_grad = lax.psum(local_grad, ('dom', 'rep'))]
    ppermute x14 -> x0, waiting for transfers between devices: 286 us -> none  [from_behind(): return lax.ppermute(block, axis, route)]
    reduce_scatter x1 -> x0, waiting for transfers between devices: 203 us -> none  [shards(): lax.psum_scatter(partial_rows, 'rep', scatter_dimension=0, tiled=True)]
    pallas_call x0 -> x1, Pallas kernels: none -> 135 us  [shards(): pl.pallas_call(layer_kernel, out_shape=(jax.ShapeDtypeStruct(cotangent.sh...]
    ppermute x14 -> x0, starting transfers between devices: 31.8 us -> none  [from_behind(): return lax.ppermute(block, axis, route)]
    unnamed x25 -> x2, local copies, waits for them, and re-layouts: 16.4 us -> 3.83 us
  transfers between devices with their start and end apart: 16 -> 0, of which waited for: 16 -> 0; matrix products, arithmetic and copies ran while one was open for 1% -> 0% of each run, Pallas kernels for 0% -> 0%
where the time goes in v2:
time: 140 us
  Pallas kernels  135 us (96%)
  local copies, waits for them, and re-layouts  3.83 us (3%)
    pallas_call x1, Pallas kernels, shards(): pl.pallas_call(layer_kernel, out_shape=(jax.ShapeDtypeStruct(cotangent.sh...  135 us
    unnamed x2, local copies, waits for them, and re-layouts  3.83 us

profile of v2, /device:TPU:1, one launch (start us, length us, event | category | flops | bytes accessed | tf_op | source)
XLA Modules:
  0.0 140.0 jit_solution(12160513738589337401)
XLA Ops:
  1.3 134.8 %layer.1 = (bf16[128,512]{1,0:T(8,128)(2,1)}, f32[512,512]{1,0:T(8,128)}) custom-call(bf16[8,128,512]{2,1,0:T(8,128)(2,1)} %bitcast.1, bf16[48,128,128]{2,1,0:T(8,128)(2,1)} %tiles.1, s32[48]{0:T(128)} %rows.1, s32[48]{0:T(128)} %cols.1, s32[1]{0:T(128)S(6)} %copy.11.count, bf16[512,512]{1,0:T(8,128)(2,1)} %weight_in.1, bf16[128,512]{1,0:T(8,128)(2,1)} %cotangent_in.1), custom_call_target="tpu_custom_call" | custom-call | tf_op jit(solution)/shard_map/layer/pallas_call | solution.py:535
  136.1 1.6 %copy.12 = bf16[128,512]{1,0:T(8,128)(2,1)} copy(bf16[128,512]{1,0:T(8,128)(2,1)} %get-tuple-element.4) | data formatting | bytes 262144
  137.7 2.3 %copy.13 = f32[512,512]{1,0:T(8,128)} copy(f32[512,512]{1,0:T(8,128)} %get-tuple-element.5) | data formatting | bytes 2097152

commit v3 on v2

v3 whole, which is shorter than its diff:
```python
import types

import jax
import jax.numpy as jnp
from jax import lax
from jax.experimental import pallas as pl
from jax.experimental.pallas import tpu as pltpu
from jax.sharding import PartitionSpec as P

MESH = pl.DeviceIdType.MESH
BF16 = jnp.bfloat16
F32 = jnp.float32
I32 = jnp.int32

WIDTHS = (256, 256)
ALONE, BOTH, FROM_Y = range(3)
SLOTS = 48
PIECES = 3
SLOT_STEP = 8
FAR_FIRST = sorted(
    [(dx, dy) for dx in range(4) for dy in range(4) if dx or dy],
    key=lambda d: -min(d[0], 4 - d[0]) - min(d[1], 4 - d[1]),
)


def at(x, y, zl, zh, core):
    return zl * 8 + x * 2 + core, zh * 4 + y


def hosted(x, y, zh, core):
    c = (2 * x + core + 16 - 4 * zh - y) % 8
    member = ((y + 1) // 2) % 2
    return c // 2, (1 - c % 2) * member + (c % 2) * (3 - member)


def set_of(host_x, host_y, zh, core):
    natural_core = host_y // 2
    member = (1 - natural_core) * host_y + natural_core * (3 - host_y)
    other = (core + natural_core) % 2
    y = (1 - other) * 2 * member + other * (3 - 2 * member)
    return ((2 * host_x + natural_core + 4 * zh + y - core) // 2) % 4, y


def place():
    dom, rep = lax.axis_index("dom"), lax.axis_index("rep")
    return (dom // 2) % 4, rep % 4, dom // 8, rep // 4, dom % 2


def z_neighbour(x, y, zl, zh, core, distance):
    z = (zh * 8 + zl + distance + 16) % 16
    return at(x, y, z % 8, z // 8, core)


def signal(device):
    pl.semaphore_signal(pltpu.get_barrier_semaphore(), inc=1, device_id=device, device_id_type=MESH)


def remote(src, dst, send, recv, device):
    return pltpu.make_async_remote_copy(
        src_ref=src, dst_ref=dst, send_sem=send, recv_sem=recv, device_id=device, device_id_type=MESH
    )


def when_not(condition, action):
    pl.when(jnp.logical_not(condition))(action)


def sort_slots(rows, cols, count, numbers):
    shape = (SLOTS, SLOTS)
    sub = lax.broadcasted_iota(I32, shape, 0).astype(F32)
    lane = lax.broadcasted_iota(I32, shape, 1).astype(F32)
    eye = (sub == lane).astype(F32)

    def column(row):
        return jnp.sum(eye * row, axis=1, keepdims=True)

    live = lane[:1] < count[...].reshape(1, 1).astype(F32)
    key = jnp.where(live, rows[...].reshape(1, SLOTS).astype(F32), 8.0)
    col = cols[...].reshape(1, SLOTS)
    block = ((col >> 6) * 8 + (col & 7)).astype(F32)
    unique = key * 64.0 + lane[:1]
    key_column = column(key)
    rank = jnp.sum((unique < column(unique)).astype(F32), axis=1, keepdims=True)
    chosen = (rank == lane).astype(F32)
    after = (rank + 1.0 == lane).astype(F32)
    sorted_key = jnp.sum(chosen * key_column, axis=0, keepdims=True)
    key_before = jnp.sum(after * key_column, axis=0, keepdims=True)
    numbers[0:1, 0:SLOTS] = jnp.sum(chosen * sub, axis=0, keepdims=True).astype(I32)
    numbers[1:2, 0:SLOTS] = jnp.sum(chosen * column(block), axis=0, keepdims=True).astype(I32)
    numbers[2:3, 0:SLOTS] = (sorted_key == key_before).astype(I32)
    ends = jnp.where(key_column == lane, rank + 1.0, 0.0)
    numbers[3:4, 0:SLOTS] = jnp.max(ends, axis=0, keepdims=True).astype(I32)


def scratch():
    vmem, sems = pltpu.VMEM, pltpu.SemaphoreType.DMA
    chunks = len(WIDTHS)
    names = {
        "numbers": vmem((8, 128), I32),
        "numbers_in": vmem((8, 128), I32),
        "own_table": pltpu.SMEM((8, 128), I32),
        "table": pltpu.SMEM((8, 128), I32),
        "tiles": vmem((SLOTS, 128, 128), BF16),
        "sorted_tiles": vmem((SLOTS, 128, 128), BF16),
        "tile_set": vmem((SLOTS, 128, 128), BF16),
        "weight": vmem((512, 512), BF16),
        "cotangent": vmem((128, 512), BF16),
        "load_sems": sems((2,)),
        "agg": vmem((2, 128, 512), BF16),
        "slope": vmem((2, 128, 512), BF16),
        "grad": vmem((16, 16, 512), BF16),
        "grad_in": vmem((16, 16, 512), BF16),
        "piece": vmem((8, 8, 128), F32),
        "piece_in": vmem((16, 8, 128), F32),
        "total": vmem((8, 128), F32),
        "total_in": vmem((8, 8, 128), F32),
        "whole": vmem((2, 16, 16, 512), BF16),
        "set_send": sems((PIECES + 1,)),
        "set_recv": sems((PIECES + 1,)),
        "local_sems": sems((3,)),
        "own_send": sems((chunks, 2)),
        "own_recv": sems((chunks, 2)),
        "ring_send": sems((chunks, 2, 4, 2)),
        "ring_recv": sems((chunks, 2, 4, 2)),
        "y_send": sems((chunks, 8)),
        "y_recv": sems((chunks, 8)),
        "pair_send": sems((chunks, 8, 3)),
        "pair_recv": sems((chunks, 8, 3)),
        "plane_send": sems((chunks, 4)),
        "plane_recv": sems((chunks, 4)),
        "z_send": sems((chunks,)),
        "z_recv": sems((chunks,)),
        "agg_send": sems((chunks,)),
        "agg_recv": sems((chunks,)),
        "slope_sems": sems((2,)),
        "grad_send": sems((16,)),
        "grad_recv": sems((16,)),
        "piece_send": sems((16,)),
        "piece_recv": sems((16,)),
        "total_send": sems((8,)),
        "total_recv": sems((8,)),
        "whole_send": sems((16,)),
        "whole_recv": sems((16,)),
        "last_sems": sems((2,)),
    }
    for q, width in enumerate(WIDTHS):
        names["blocks%d" % q] = vmem((64, 128, width), BF16)
        names["products%d" % q] = vmem((SLOTS + 1, 128, width), F32)
        names["partial%d" % q] = vmem((2, 4, 128, width), BF16)
        names["plane_in%d" % q] = vmem((4, 2, 128, width), BF16)
        names["z_out%d" % q] = vmem((128, width), BF16)
        names["z_in%d" % q] = vmem((128, width), BF16)
        names["own%d" % q] = vmem((128, width), F32)
    return names


def layer_kernel(features, tiles_in, rows, cols, count, weight_in, cotangent_in, node_out, weight_grad, *refs):
    s = types.SimpleNamespace(**dict(zip(scratch(), refs)))
    chunks = len(WIDTHS)
    starts = [sum(WIDTHS[:q]) for q in range(chunks)]

    def of(name, q):
        return getattr(s, name + str(q))

    x, y, zl, zh, core = place()
    z = zh * 8 + zl
    spot = x * 4 + y
    sibling = at(x, y, zl, zh, 1 - core)
    up = z_neighbour(x, y, zl, zh, core, 1)
    down = z_neighbour(x, y, zl, zh, core, -1)
    natural_core = y // 2
    is_source = core == natural_core
    member = y % 2
    y_pair = at(x, y + 1 - 2 * member, zl, zh, core)

    def in_plane(step):
        return at((x + step[0]) % 4, (y + step[1]) % 4, zl, zh, core)

    def spot_at(step):
        return (x + step[0]) % 4 * 4 + (y + step[1]) % 4

    weight, cotangent = s.weight, s.cotangent
    loads = [
        pltpu.make_async_copy(weight_in, weight, s.load_sems.at[0]),
        pltpu.make_async_copy(cotangent_in, cotangent, s.load_sems.at[1]),
    ]
    load_tiles = pltpu.make_async_copy(tiles_in, s.tiles, s.local_sems.at[0])
    load_tiles.start()

    signal(up)
    signal(down)
    signal(sibling)
    for distance in (8, 7, 9, 6, 10, 5, 11, 4, 12, 3, 13, 2, 14):
        signal(z_neighbour(x, y, zl, zh, core, distance))
    for step in FAR_FIRST:
        signal(in_plane(step))
    sort_slots(rows, cols, count, s.numbers)
    to_own_table = pltpu.make_async_copy(s.numbers, s.own_table, s.local_sems.at[1])
    to_own_table.start()
    for q in range(chunks):
        of("products", q)[0] = jnp.zeros((128, WIDTHS[q]), F32)
    load_tiles.wait()
    to_own_table.wait()
    for load in loads:
        load.start()

    def entry(table, row, place, top):
        return jnp.minimum(jnp.maximum(table[row, place], 0), top)

    def place_tile(j, carry):
        s.sorted_tiles[j] = s.tiles[entry(s.own_table, 0, j, SLOTS - 1)]
        return carry

    lax.fori_loop(0, SLOTS, place_tile, 0, unroll=2)
    pl.semaphore_wait(pltpu.get_barrier_semaphore(), 31)

    def block_rows(distance, of_core):
        return (zl + distance + 8) % 8 * 8 + of_core * 4

    def block_part(q, distance, unit, of_core):
        row = block_rows(distance, of_core)
        row = row + (member if unit == ALONE else 2 if unit == BOTH else 1 - member)
        return of("blocks", q).at[pl.ds(row, 2 if unit == BOTH else 1)]

    def own_part(q, of_core):
        columns = pl.ds(starts[q], WIDTHS[q])
        return features.at[pl.ds(of_core * 4, 4), :, columns], of("blocks", q).at[pl.ds(block_rows(0, of_core), 4)]

    def own_local(q, of_core):
        return pltpu.make_async_copy(*own_part(q, of_core), s.own_recv.at[q, of_core])

    def own_remote(q, of_core):
        return remote(*own_part(q, of_core), s.own_send.at[q, of_core], s.own_recv.at[q, of_core], sibling)

    def send_own(q):
        @pl.when(is_source)
        def _():
            own_remote(q, 1 - core).start()
            own_local(q, core).start()
            own_remote(q, core).start()
            own_local(q, 1 - core).start()

    def hop(q, step, unit, upward):
        ref = block_part(q, -step if upward else step, unit, core)
        way = 0 if upward else 1
        return remote(
            ref, ref, s.ring_send.at[q, way, step, unit], s.ring_recv.at[q, way, step, unit], up if upward else down
        )

    def arrival(q, step, unit, upward):
        ref = block_part(q, -step - 1 if upward else step + 1, unit, core)
        way = 0 if upward else 1
        return remote(ref, ref, s.ring_send.at[q, way, step, unit], s.ring_recv.at[q, way, step, unit], sibling)

    def y_copy(q, distance, unit):
        ref = block_part(q, distance, unit, core)
        return remote(ref, ref, s.y_send.at[q, distance + 4], s.y_recv.at[q, distance + 4], y_pair)

    def pair_copy(q, distance, unit, of_core):
        ref = block_part(q, distance, unit, of_core)
        return remote(ref, ref, s.pair_send.at[q, distance + 4, unit], s.pair_recv.at[q, distance + 4, unit], sibling)

    def hops(q, unit, upward):
        return 4 if (unit == (ALONE if q % 2 == 0 else BOTH)) == upward else 3

    def own_event(q):
        own_local(q, core).wait()
        for unit in (ALONE, BOTH):
            hop(q, 0, unit, True).start()
            hop(q, 0, unit, False).start()

    def ring_event(q, step, unit, upward):
        arrival(q, step, unit, upward).wait_recv()
        if step + 1 < hops(q, unit, upward):
            hop(q, step + 1, unit, upward).start()
        distance = -step - 1 if upward or step == 3 else step + 1
        if unit == ALONE:
            y_copy(q, distance, ALONE).start()
        pair_copy(q, distance, unit, core).start()

    def y_event(q, distance):
        y_copy(q, distance, FROM_Y).wait_recv()
        pair_copy(q, distance, FROM_Y, core).start()

    def ring_events(q, step):
        return [
            lambda unit=unit, upward=upward: ring_event(q, step, unit, upward)
            for unit in (ALONE, BOTH)
            for upward in (True, False)
            if step < hops(q, unit, upward)
        ]

    def y_events(q, step):
        distances = (-4,) if step == 3 else (-step - 1, step + 1)
        return [lambda distance=distance: y_event(q, distance) for distance in distances]

    def pair_arrivals(q):
        own_local(q, 1 - core).wait()
        for distance in (-1, 1, -2, 2, -3, 3, -4):
            for unit in (ALONE, BOTH, FROM_Y):
                pair_copy(q, distance, unit, 1 - core).wait_recv()

    host_x, host_y = hosted(x, y, zh, core)
    stays = (host_x + 4 - x) % 4 + (host_y + 4 - y) % 4 == 0
    host = at(host_x, host_y, zl, zh, core)
    per_piece = SLOTS // PIECES
    set_parts = [(s.numbers, s.numbers_in)] + [
        (s.sorted_tiles.at[pl.ds(i * per_piece, per_piece)], s.tile_set.at[pl.ds(i * per_piece, per_piece)])
        for i in range(PIECES)
    ]

    def set_remote(i):
        return remote(*set_parts[i], s.set_send.at[i], s.set_recv.at[i], host)

    def set_local(i):
        return pltpu.make_async_copy(*set_parts[i], s.set_recv.at[i])

    def send_set():
        @pl.when(stays)
        def _():
            for i in range(PIECES + 1):
                set_local(i).start()

        @pl.when(jnp.logical_not(stays))
        def _():
            for i in range(PIECES + 1):
                set_remote(i).start()

    def receive_table():
        set_local(0).wait()
        to_table = pltpu.make_async_copy(s.numbers_in, s.table, s.local_sems.at[2])
        to_table.start()
        to_table.wait()

    def receive_piece(i):
        set_local(i + 1).wait()

    def multiply(q, first):
        def four(i, carry):
            base = first + 4 * i
            total = of("products", q)[base]
            for j in range(4):
                block = of("blocks", q)[entry(s.table, 1, base + j, 63)]
                product = jnp.dot(s.tile_set[base + j], block, preferred_element_type=F32)
                total = product + s.table[2, base + j].astype(F32) * total
                of("products", q)[base + j + 1] = total
            return carry

        lax.fori_loop(0, SLOT_STEP // 4, four, 0)

    def multiplies(q, pieces):
        slots = range(pieces[0] * per_piece, (pieces[-1] + 1) * per_piece, SLOT_STEP)
        return [lambda first=first: multiply(q, first) for first in slots]

    set_x, set_y = set_of(x, y, zh, core)
    here = (set_x + 4 - x) % 4 == 0

    def to_owner(q, distance):
        there = (y + distance) % 4
        return remote(
            of("partial", q).at[:, there], of("plane_in", q).at[set_y], s.plane_send.at[q, distance],
            s.plane_recv.at[q, set_y], at(set_x, there, zl, zh, core),
        )

    def send_partial(q):
        for t in range(8):
            of("partial", q)[t // 4, t % 4] = of("products", q)[entry(s.table, 3, t, SLOTS)].astype(BF16)
        for distance in (2, 1, 3):
            to_owner(q, distance).start()

        @pl.when(here)
        def _():
            pltpu.make_async_copy(
                of("partial", q).at[:, y], of("plane_in", q).at[set_y], s.plane_recv.at[q, set_y]
            ).start()

        when_not(here, lambda: to_owner(q, 0).start())

    def across(q):
        return remote(
            of("z_out", q), of("z_in", q), s.z_send.at[q], s.z_recv.at[q], z_neighbour(x, y, zl, zh, core, 8)
        )

    def sum_plane(q):
        for member in range(4):
            ref = of("plane_in", q).at[member]
            remote(ref, ref, s.plane_send.at[q, 0], s.plane_recv.at[q, member], sibling).wait_recv()

        def summed(part):
            result = of("plane_in", q)[0, part].astype(F32)
            for member in range(1, 4):
                result += of("plane_in", q)[member, part].astype(F32)
            return result

        of("z_out", q)[...] = summed(1 - zh).astype(BF16)
        across(q).start()
        of("own", q)[...] = summed(zh)

    def agg_copy(q, of_core):
        ref = s.agg.at[of_core, :, pl.ds(starts[q], WIDTHS[q])]
        return remote(ref, ref, s.agg_send.at[q], s.agg_recv.at[q], sibling)

    def aggregate(q):
        across(q).wait_recv()
        mine = (of("own", q)[...] + of("z_in", q)[...].astype(F32)).astype(BF16)
        s.agg[core, :, starts[q] : starts[q] + WIDTHS[q]] = mine
        agg_copy(q, core).start()
        return jnp.dot(mine, weight[starts[q] : starts[q] + WIDTHS[q], :], preferred_element_type=F32)

    slots = [[] for _ in range(2 * chunks + 4)]
    for q in range(chunks):
        slots[2 * q].append(lambda q=q: own_event(q))
        for step in range(4):
            slots[2 * q + 1 + step] += ring_events(q, step)
            slots[2 * q + 2 + step] += y_events(q, step)

    send_own(0)
    send_set()
    for q in range(1, chunks):
        send_own(q)
    work = []
    for slot, events in enumerate(slots):
        complete = slot // 2 - 3
        if slot == 6:
            work += [lambda: pair_arrivals(0), receive_table, lambda: receive_piece(0)] + multiplies(0, (0,))
            work += [lambda: receive_piece(1)] + multiplies(0, (1,))
        elif slot % 2 == 0 and 0 < complete < chunks - 1:
            work += [lambda q=complete: pair_arrivals(q)] + multiplies(complete, (0, 1))
        for event in events:
            event()
            if work:
                work.pop(0)()
    for item in work:
        item()
    receive_piece(2)
    for q in range(chunks - 1):
        for item in multiplies(q, (2,)):
            item()
        send_partial(q)
    pair_arrivals(chunks - 1)
    for item in multiplies(chunks - 1, (0, 1, 2)):
        item()
    send_partial(chunks - 1)
    for q in range(chunks - 1):
        sum_plane(q)
    for load in loads:
        load.wait()
    pre = aggregate(0)
    for q in range(1, chunks - 1):
        pre += aggregate(q)
    sum_plane(chunks - 1)
    pre += aggregate(chunks - 1)

    sigma = jax.nn.sigmoid(pre)
    s.slope[core] = (cotangent[...].astype(F32) * sigma * (1.0 + pre * (1.0 - sigma))).astype(BF16)
    slope_copy = remote(s.slope.at[core], s.slope.at[core], s.slope_sems.at[0], s.slope_sems.at[1], sibling)
    slope_copy.start()
    node_out[...] = (pre * sigma).astype(node_out.dtype)
    for q in range(chunks):
        agg_copy(q, 1 - core).wait_recv()
    slope_copy.wait_recv()

    columns = pl.ds(pl.multiple_of(core * 256, 256), 256)
    local = lax.dot_general(
        s.agg[:, :, columns].reshape(256, 256), s.slope[...].reshape(256, 512),
        (((0,), (0,)), ((), ())), preferred_element_type=F32,
    )
    s.grad[...] = local.reshape(16, 16, 512).astype(BF16)

    def grad_copy(step):
        there = spot_at(step)
        return remote(
            s.grad.at[there], s.grad_in.at[spot], s.grad_send.at[4 * step[0] + step[1]], s.grad_recv.at[spot],
            in_plane(step),
        )

    for step in FAR_FIRST:
        grad_copy(step).start()
    rows_sum = s.grad[spot].astype(F32)
    for step in reversed(FAR_FIRST):
        there = spot_at(step)
        ref = s.grad_in.at[there]
        remote(ref, ref, s.grad_send.at[0], s.grad_recv.at[there], sibling).wait_recv()
        rows_sum += s.grad_in[there].astype(F32)
    for j in range(8):
        s.piece[j] = rows_sum[8 * (j // 4) : 8 * (j // 4) + 8, 128 * (j % 4) : 128 * (j % 4) + 128]

    def piece_copy(distance):
        there = (z + distance) % 16
        return remote(
            s.piece.at[there % 8], s.piece_in.at[z], s.piece_send.at[distance], s.piece_recv.at[z],
            z_neighbour(x, y, zl, zh, core, distance),
        )

    for distance in (8, 7, 9, 6, 10, 5, 11, 4, 12, 3, 13, 2, 14, 1, 15):
        piece_copy(distance).start()
    s.piece_in[z] = s.piece[zl]
    for distance in range(1, 16):
        there = (z + distance) % 16
        ref = s.piece_in.at[there]
        remote(ref, ref, s.piece_send.at[0], s.piece_recv.at[there], sibling).wait_recv()
    result = s.piece_in[0]
    for j in range(1, 16):
        result += s.piece_in[j]
    s.total[...] = result
    s.total_in[zl] = result

    def total_copy(distance):
        return remote(
            s.total, s.total_in.at[zl], s.total_send.at[distance + 3], s.total_recv.at[zl],
            z_neighbour(x, y, zl, zh, core, distance),
        )

    near = (4, -3, 3, -2, 2, -1, 1)
    for distance in near:
        total_copy(distance).start()
    for distance in range(1, 8):
        there = (zl + distance) % 8
        remote(s.total, s.total_in.at[there], s.total_send.at[0], s.total_recv.at[there], sibling).wait_recv()
    upper = jnp.concatenate([s.total_in[j] for j in range(4)], axis=1)
    lower = jnp.concatenate([s.total_in[j] for j in range(4, 8)], axis=1)
    s.whole[core, spot] = jnp.concatenate([upper, lower], axis=0).astype(BF16)

    def whole_copy(step):
        ref = s.whole.at[core, spot]
        return remote(ref, ref, s.whole_send.at[4 * step[0] + step[1]], s.whole_recv.at[spot], in_plane(step))

    for step in FAR_FIRST:
        whole_copy(step).start()
    for step in reversed(FAR_FIRST):
        there = spot_at(step)
        ref = s.whole.at[core, there]
        remote(ref, ref, s.whole_send.at[0], s.whole_recv.at[there], sibling).wait_recv()
    final = remote(s.whole.at[core], s.whole.at[core], s.last_sems.at[0], s.last_sems.at[1], sibling)
    final.start()
    final.wait_recv()
    weight_grad[...] = s.whole[...].reshape(512, 512)

    for q in range(chunks):
        @pl.when(is_source)
        def _():
            own_remote(q, 0).wait_send()
            own_remote(q, 1).wait_send()

        for unit in (ALONE, BOTH):
            for upward in (True, False):
                for step in range(hops(q, unit, upward)):
                    hop(q, step, unit, upward).wait_send()
        for distance in (-4, -3, -2, -1, 1, 2, 3):
            y_copy(q, distance, ALONE).wait_send()
            for unit in (ALONE, BOTH, FROM_Y):
                pair_copy(q, distance, unit, core).wait_send()
        for distance in (1, 2, 3):
            to_owner(q, distance).wait_send()
        when_not(here, lambda: to_owner(q, 0).wait_send())
        across(q).wait_send()
        agg_copy(q, core).wait_send()

    @pl.when(jnp.logical_not(stays))
    def _():
        for i in range(PIECES + 1):
            set_remote(i).wait_send()

    slope_copy.wait_send()
    for step in FAR_FIRST:
        grad_copy(step).wait_send()
        whole_copy(step).wait_send()
    for distance in range(1, 16):
        piece_copy(distance).wait_send()
    for distance in near:
        total_copy(distance).wait_send()
    final.wait_send()


def shards(features, tiles, tile_rows, tile_cols, tile_count, weight, cotangent):
    vmem = pl.BlockSpec(memory_space=pltpu.VMEM)
    anywhere = pl.BlockSpec(memory_space=pl.ANY)
    node_out, weight_grad = pl.pallas_call(
        layer_kernel,
        out_shape=(
            jax.ShapeDtypeStruct(cotangent.shape, BF16),
            jax.ShapeDtypeStruct(weight.shape, BF16),
        ),
        in_specs=[anywhere, anywhere, vmem, vmem, vmem, anywhere, anywhere],
        out_specs=(vmem, vmem),
        scratch_shapes=list(scratch().values()),
        compiler_params=pltpu.CompilerParams(
            collective_id=0, has_side_effects=True, vmem_limit_bytes=60 * 2**20
        ),
        name="layer",
    )(
        features.reshape(8, 128, 512), tiles, tile_rows, tile_cols, tile_count, weight, cotangent,
    )
    return node_out, weight_grad.astype(F32)


def solution(mesh):
    in_specs = (
        P("dom", None),
        P(("dom", "rep"), None, None),
        P(("dom", "rep")),
        P(("dom", "rep")),
        P(("dom", "rep")),
        P(),
        P(("dom", "rep"), None),
    )
    out_specs = (P(("dom", "rep"), None), P())
    return jax.shard_map(shards, mesh=mesh, in_specs=in_specs, out_specs=out_specs, check_vma=False)
```

time: 140 us -> 125 us (0.89)
  Pallas kernels: 135 us -> 121 us
  local copies, waits for them, and re-layouts: 3.83 us -> 0.66 us
  other arithmetic: 0 us -> 2.18 us
    pallas_call x1, Pallas kernels: 135 us -> 121 us  [shards(): pl.pallas_call(layer_kernel, out_shape=(jax.ShapeDtypeStruct(cotangent.sh...]
    unnamed x2 -> x3, local copies, waits for them, and re-layouts: 3.83 us -> 0.66 us
    convert_element_type x0 -> x1, other arithmetic: none -> 2.18 us  [shards(): return (node_out, weight_grad.astype(F32))]
where the time goes in v3:
time: 125 us
  Pallas kernels  121 us (97%)
  other arithmetic  2.18 us (2%)
  between operations  1.29 us (1%)
    pallas_call x1, Pallas kernels, shards(): pl.pallas_call(layer_kernel, out_shape=(jax.ShapeDtypeStruct(cotangent.sh...  121 us

profile of v3, /device:TPU:1, one launch (start us, length us, event | category | flops | bytes accessed | tf_op | source)
XLA Modules:
  0.0 125.2 jit_solution(3504152810786838932)
XLA Ops:
  1.3 121.1 %layer.1 = (bf16[128,512]{1,0:T(8,128)(2,1)}, bf16[512,512]{1,0:T(8,128)(2,1)}) custom-call(bf16[8,128,512]{2,1,0:T(8,128)(2,1)} %bitcast.1, bf16[48,128,128]{2,1,0:T(8,128)(2,1)} %tiles_in.1, s32[48]{0:T(128)} %rows.1, s32[48]{0:T(128)} %cols.1, s32[1]{0:T(128)S(6)} %copy.10.count, bf16[512,512]{1,0:T(8,128)(2,1)} %weight_in.1, bf16[128,512]{1,0:T(8,128)(2,1)} %cotangent_in.1), custom_call_target="tpu_custom_call" | custom-call | tf_op jit(solution)/shard_map/layer/pallas_call | solution.py:578
  122.4 0.0 copy-start
  122.4 2.2 %convert_element_type.3 = f32[512,512]{1,0:T(8,128)} convert(bf16[512,512]{1,0:T(8,128)(2,1)} %get-tuple-element.5) | non-fusion elementwise | flops 262144 | bytes 1572864 | tf_op jit(solution)/shard_map/convert_element_type | solution.py:594
  124.6 0.0 copy-done
  124.6 0.7 copy.11
Async XLA Ops:
  122.4 2.2 %copy-start = (bf16[128,512]{1,0:T(8,128)(2,1)S(1)}, bf16[128,512]{1,0:T(8,128)(2,1)}, u32[]{:S(2)}) copy-start(bf16[128,512]{1,0:T(8,128)(2,1)} %get-tuple-element.8) | copy-start | bytes 393220

commit v4 on v3

--- a/solution.py
+++ b/solution.py
@@ -14,6 +14,7 @@
 
 WIDTHS = (256, 256)
 ALONE, BOTH, FROM_Y = range(3)
+SUMS = [(q, first) for q, width in enumerate(WIDTHS) for first in range(0, width, 128)]
 SLOTS = 48
 PIECES = 3
 SLOT_STEP = 8
@@ -106,6 +107,7 @@
         "weight": vmem((512, 512), BF16),
         "cotangent": vmem((128, 512), BF16),
         "load_sems": sems((2,)),
+        "line_sems": pltpu.SemaphoreType.REGULAR((3,)),
         "agg": vmem((2, 128, 512), BF16),
         "slope": vmem((2, 128, 512), BF16),
         "grad": vmem((16, 16, 512), BF16),
@@ -124,14 +126,15 @@
         "ring_recv": sems((chunks, 2, 4, 2)),
         "y_send": sems((chunks, 8)),
         "y_recv": sems((chunks, 8)),
+        "y_other_send": sems((chunks,)),
         "pair_send": sems((chunks, 8, 3)),
         "pair_recv": sems((chunks, 8, 3)),
-        "plane_send": sems((chunks, 4)),
-        "plane_recv": sems((chunks, 4)),
-        "z_send": sems((chunks,)),
-        "z_recv": sems((chunks,)),
-        "agg_send": sems((chunks,)),
-        "agg_recv": sems((chunks,)),
+        "plane_send": sems((len(SUMS), 4)),
+        "plane_recv": sems((len(SUMS), 4)),
+        "z_send": sems((len(SUMS),)),
+        "z_recv": sems((len(SUMS),)),
+        "agg_send": sems((len(SUMS),)),
+        "agg_recv": sems((len(SUMS),)),
         "slope_sems": sems((2,)),
         "grad_send": sems((16,)),
         "grad_recv": sems((16,)),
@@ -141,16 +144,18 @@
         "total_recv": sems((8,)),
         "whole_send": sems((16,)),
         "whole_recv": sems((16,)),
-        "last_sems": sems((2,)),
+        "last_send": sems((16,)),
+        "last_recv": sems((16,)),
     }
     for q, width in enumerate(WIDTHS):
         names["blocks%d" % q] = vmem((64, 128, width), BF16)
         names["products%d" % q] = vmem((SLOTS + 1, 128, width), F32)
-        names["partial%d" % q] = vmem((2, 4, 128, width), BF16)
-        names["plane_in%d" % q] = vmem((4, 2, 128, width), BF16)
-        names["z_out%d" % q] = vmem((128, width), BF16)
-        names["z_in%d" % q] = vmem((128, width), BF16)
-        names["own%d" % q] = vmem((128, width), F32)
+    for part in range(len(SUMS)):
+        names["partial%d" % part] = vmem((2, 4, 128, 128), BF16)
+        names["plane_in%d" % part] = vmem((4, 2, 128, 128), BF16)
+        names["z_out%d" % part] = vmem((128, 128), BF16)
+        names["z_in%d" % part] = vmem((128, 128), BF16)
+        names["own%d" % part] = vmem((128, 128), F32)
     return names
 
 
@@ -172,6 +177,7 @@
     is_source = core == natural_core
     member = y % 2
     y_pair = at(x, y + 1 - 2 * member, zl, zh, core)
+    y_pair_other = at(x, y + 1 - 2 * member, zl, zh, 1 - core)
 
     def in_plane(step):
         return at((x + step[0]) % 4, (y + step[1]) % 4, zl, zh, core)
@@ -190,29 +196,35 @@
     signal(up)
     signal(down)
     signal(sibling)
-    for distance in (8, 7, 9, 6, 10, 5, 11, 4, 12, 3, 13, 2, 14):
-        signal(z_neighbour(x, y, zl, zh, core, distance))
+    signal(y_pair_other)
     for step in FAR_FIRST:
         signal(in_plane(step))
+    def entry(table, row, place, top):
+        return jnp.minimum(jnp.maximum(table[row, place], 0), top)
+
+    def place_tile(j, carry):
+        s.sorted_tiles[j] = s.tiles[entry(s.own_table, 0, j, SLOTS - 1)]
+        return carry
+
     sort_slots(rows, cols, count, s.numbers)
     to_own_table = pltpu.make_async_copy(s.numbers, s.own_table, s.local_sems.at[1])
     to_own_table.start()
-    for q in range(chunks):
-        of("products", q)[0] = jnp.zeros((128, WIDTHS[q]), F32)
     load_tiles.wait()
     to_own_table.wait()
-    for load in loads:
-        load.start()
-
-    def entry(table, row, place, top):
-        return jnp.minimum(jnp.maximum(table[row, place], 0), top)
-
-    def place_tile(j, carry):
-        s.sorted_tiles[j] = s.tiles[entry(s.own_table, 0, j, SLOTS - 1)]
-        return carry
-
     lax.fori_loop(0, SLOTS, place_tile, 0, unroll=2)
-    pl.semaphore_wait(pltpu.get_barrier_semaphore(), 31)
+
+    pl.semaphore_wait(pltpu.get_barrier_semaphore(), 19)
+
+    def greet(i):
+        for distance in (2**i, -(2**i)):
+            pl.semaphore_signal(
+                s.line_sems.at[i], inc=1, device_id=z_neighbour(x, y, zl, zh, core, distance), device_id_type=MESH
+            )
+
+    def greeted(i):
+        pl.semaphore_wait(s.line_sems.at[i], 2)
+
+    greet(0)
 
     def block_rows(distance, of_core):
         return (zl + distance + 8) % 8 * 8 + of_core * 4
@@ -256,6 +268,10 @@
         ref = block_part(q, distance, unit, core)
         return remote(ref, ref, s.y_send.at[q, distance + 4], s.y_recv.at[q, distance + 4], y_pair)
 
+    def y_other_copy(q):
+        ref = block_part(q, -4, ALONE, core)
+        return remote(ref, ref, s.y_other_send.at[q], s.pair_recv.at[q, 0, FROM_Y], y_pair_other)
+
     def pair_copy(q, distance, unit, of_core):
         ref = block_part(q, distance, unit, of_core)
         return remote(ref, ref, s.pair_send.at[q, distance + 4, unit], s.pair_recv.at[q, distance + 4, unit], sibling)
@@ -276,11 +292,14 @@
         distance = -step - 1 if upward or step == 3 else step + 1
         if unit == ALONE:
             y_copy(q, distance, ALONE).start()
+            if distance == -4:
+                y_other_copy(q).start()
         pair_copy(q, distance, unit, core).start()
 
     def y_event(q, distance):
         y_copy(q, distance, FROM_Y).wait_recv()
-        pair_copy(q, distance, FROM_Y, core).start()
+        if distance != -4:
+            pair_copy(q, distance, FROM_Y, core).start()
 
     def ring_events(q, step):
         return [
@@ -355,57 +374,94 @@
     set_x, set_y = set_of(x, y, zh, core)
     here = (set_x + 4 - x) % 4 == 0
 
-    def to_owner(q, distance):
+    def to_owner(part, distance):
         there = (y + distance) % 4
         return remote(
-            of("partial", q).at[:, there], of("plane_in", q).at[set_y], s.plane_send.at[q, distance],
-            s.plane_recv.at[q, set_y], at(set_x, there, zl, zh, core),
+            of("partial", part).at[:, there], of("plane_in", part).at[set_y], s.plane_send.at[part, distance],
+            s.plane_recv.at[part, set_y], at(set_x, there, zl, zh, core),
         )
 
-    def send_partial(q):
+    def send_partial(part):
+        q, first = SUMS[part]
         for t in range(8):
-            of("partial", q)[t // 4, t % 4] = of("products", q)[entry(s.table, 3, t, SLOTS)].astype(BF16)
+            sums = of("products", q)[entry(s.table, 3, t, SLOTS), :, first : first + 128]
+            of("partial", part)[t // 4, t % 4] = sums.astype(BF16)
         for distance in (2, 1, 3):
-            to_owner(q, distance).start()
+            to_owner(part, distance).start()
 
         @pl.when(here)
         def _():
             pltpu.make_async_copy(
-                of("partial", q).at[:, y], of("plane_in", q).at[set_y], s.plane_recv.at[q, set_y]
+                of("partial", part).at[:, y], of("plane_in", part).at[set_y], s.plane_recv.at[part, set_y]
             ).start()
 
-        when_not(here, lambda: to_owner(q, 0).start())
-
-    def across(q):
+        when_not(here, lambda: to_owner(part, 0).start())
+
+    def across(part):
         return remote(
-            of("z_out", q), of("z_in", q), s.z_send.at[q], s.z_recv.at[q], z_neighbour(x, y, zl, zh, core, 8)
+            of("z_out", part), of("z_in", part), s.z_send.at[part], s.z_recv.at[part], z_neighbour(x, y, zl, zh, core, 8)
         )
 
-    def sum_plane(q):
+    def sum_plane(part):
         for member in range(4):
-            ref = of("plane_in", q).at[member]
-            remote(ref, ref, s.plane_send.at[q, 0], s.plane_recv.at[q, member], sibling).wait_recv()
-
-        def summed(part):
-            result = of("plane_in", q)[0, part].astype(F32)
+            ref = of("plane_in", part).at[member]
+            remote(ref, ref, s.plane_send.at[part, 0], s.plane_recv.at[part, member], sibling).wait_recv()
+
+        def summed(half):
+            result = of("plane_in", part)[0, half].astype(F32)
             for member in range(1, 4):
-                result += of("plane_in", q)[member, part].astype(F32)
+                result += of("plane_in", part)[member, half].astype(F32)
             return result
 
-        of("z_out", q)[...] = summed(1 - zh).astype(BF16)
-        across(q).start()
-        of("own", q)[...] = summed(zh)
-
-    def agg_copy(q, of_core):
-        ref = s.agg.at[of_core, :, pl.ds(starts[q], WIDTHS[q])]
-        return remote(ref, ref, s.agg_send.at[q], s.agg_recv.at[q], sibling)
-
-    def aggregate(q):
-        across(q).wait_recv()
-        mine = (of("own", q)[...] + of("z_in", q)[...].astype(F32)).astype(BF16)
-        s.agg[core, :, starts[q] : starts[q] + WIDTHS[q]] = mine
-        agg_copy(q, core).start()
-        return jnp.dot(mine, weight[starts[q] : starts[q] + WIDTHS[q], :], preferred_element_type=F32)
+        of("z_out", part)[...] = summed(1 - zh).astype(BF16)
+        across(part).start()
+        of("own", part)[...] = summed(zh)
+
+    def agg_copy(part, of_core):
+        ref = s.agg.at[of_core, :, pl.ds(128 * part, 128)]
+        return remote(ref, ref, s.agg_send.at[part], s.agg_recv.at[part], sibling)
+
+    def aggregate(part):
+        across(part).wait_recv()
+        mine = (of("own", part)[...] + of("z_in", part)[...].astype(F32)).astype(BF16)
+        s.agg[core, :, 128 * part : 128 * part + 128] = mine
+        agg_copy(part, core).start()
+        return jnp.dot(mine, weight[128 * part : 128 * part + 128, :], preferred_element_type=F32)
+
+    def send_sums(q):
+        for part, (of_columns, _) in enumerate(SUMS):
+            if of_columns == q:
+                send_partial(part)
+
+    def drain_features(q):
+        @pl.when(is_source)
+        def _():
+            own_remote(q, 0).wait_send()
+            own_remote(q, 1).wait_send()
+
+        for unit in (ALONE, BOTH):
+            for upward in (True, False):
+                for step in range(hops(q, unit, upward)):
+                    hop(q, step, unit, upward).wait_send()
+        for distance in (-4, -3, -2, -1, 1, 2, 3):
+            y_copy(q, distance, ALONE).wait_send()
+            for unit in (ALONE, BOTH, FROM_Y):
+                if unit != FROM_Y or distance != -4:
+                    pair_copy(q, distance, unit, core).wait_send()
+        y_other_copy(q).wait_send()
+
+    def drain_set():
+        @pl.when(jnp.logical_not(stays))
+        def _():
+            for i in range(PIECES + 1):
+                set_remote(i).wait_send()
+
+    def drain_sums(part):
+        for distance in (1, 2, 3):
+            to_owner(part, distance).wait_send()
+        when_not(here, lambda: to_owner(part, 0).wait_send())
+        across(part).wait_send()
+        agg_copy(part, core).wait_send()
 
     slots = [[] for _ in range(2 * chunks + 4)]
     for q in range(chunks):
@@ -416,11 +472,21 @@
 
     send_own(0)
     send_set()
+    for event in slots.pop(0):
+        event()
     for q in range(1, chunks):
         send_own(q)
+    for load in loads:
+        load.start()
+    for q in range(chunks):
+        of("products", q)[0] = jnp.zeros((128, WIDTHS[q]), F32)
     work = []
-    for slot, events in enumerate(slots):
+    for slot, events in enumerate(slots, 1):
         complete = slot // 2 - 3
+        if slot in (2, 4, 6):
+            greeted(slot // 2 - 1)
+            if slot < 6:
+                greet(slot // 2)
         if slot == 6:
             work += [lambda: pair_arrivals(0), receive_table, lambda: receive_piece(0)] + multiplies(0, (0,))
             work += [lambda: receive_piece(1)] + multiplies(0, (1,))
@@ -436,28 +502,29 @@
     for q in range(chunks - 1):
         for item in multiplies(q, (2,)):
             item()
-        send_partial(q)
+        send_sums(q)
     pair_arrivals(chunks - 1)
     for item in multiplies(chunks - 1, (0, 1, 2)):
         item()
-    send_partial(chunks - 1)
-    for q in range(chunks - 1):
-        sum_plane(q)
+    send_sums(chunks - 1)
+    for q in range(chunks):
+        drain_features(q)
+    drain_set()
     for load in loads:
         load.wait()
+    for part in range(len(SUMS)):
+        sum_plane(part)
     pre = aggregate(0)
-    for q in range(1, chunks - 1):
-        pre += aggregate(q)
-    sum_plane(chunks - 1)
-    pre += aggregate(chunks - 1)
+    for part in range(1, len(SUMS)):
+        pre += aggregate(part)
 
     sigma = jax.nn.sigmoid(pre)
     s.slope[core] = (cotangent[...].astype(F32) * sigma * (1.0 + pre * (1.0 - sigma))).astype(BF16)
     slope_copy = remote(s.slope.at[core], s.slope.at[core], s.slope_sems.at[0], s.slope_sems.at[1], sibling)
     slope_copy.start()
     node_out[...] = (pre * sigma).astype(node_out.dtype)
-    for q in range(chunks):
-        agg_copy(q, 1 - core).wait_recv()
+    for part in range(len(SUMS)):
+        agg_copy(part, 1 - core).wait_recv()
     slope_copy.wait_recv()
 
     columns = pl.ds(pl.multiple_of(core * 256, 256), 256)
@@ -476,6 +543,9 @@
 
     for step in FAR_FIRST:
         grad_copy(step).start()
+    slope_copy.wait_send()
+    for part in range(len(SUMS)):
+        drain_sums(part)
     rows_sum = s.grad[spot].astype(F32)
     for step in reversed(FAR_FIRST):
         there = spot_at(step)
@@ -495,6 +565,8 @@
     for distance in (8, 7, 9, 6, 10, 5, 11, 4, 12, 3, 13, 2, 14, 1, 15):
         piece_copy(distance).start()
     s.piece_in[z] = s.piece[zl]
+    for step in FAR_FIRST:
+        grad_copy(step).wait_send()
     for distance in range(1, 16):
         there = (z + distance) % 16
         ref = s.piece_in.at[there]
@@ -514,6 +586,8 @@
     near = (4, -3, 3, -2, 2, -1, 1)
     for distance in near:
         total_copy(distance).start()
+    for distance in range(1, 16):
+        piece_copy(distance).wait_send()
     for distance in range(1, 8):
         there = (zl + distance) % 8
         remote(s.total, s.total_in.at[there], s.total_send.at[0], s.total_recv.at[there], sibling).wait_recv()
@@ -525,51 +599,28 @@
         ref = s.whole.at[core, spot]
         return remote(ref, ref, s.whole_send.at[4 * step[0] + step[1]], s.whole_recv.at[spot], in_plane(step))
 
+    def last_copy(n, of_core):
+        ref = s.whole.at[of_core, n]
+        return remote(ref, ref, s.last_send.at[n], s.last_recv.at[n], sibling)
+
     for step in FAR_FIRST:
         whole_copy(step).start()
+    last_copy(spot, core).start()
+    for distance in near:
+        total_copy(distance).wait_send()
     for step in reversed(FAR_FIRST):
         there = spot_at(step)
         ref = s.whole.at[core, there]
         remote(ref, ref, s.whole_send.at[0], s.whole_recv.at[there], sibling).wait_recv()
-    final = remote(s.whole.at[core], s.whole.at[core], s.last_sems.at[0], s.last_sems.at[1], sibling)
-    final.start()
-    final.wait_recv()
+        last_copy(there, core).start()
+    for n in range(16):
+        last_copy(n, 1 - core).wait_recv()
     weight_grad[...] = s.whole[...].reshape(512, 512)
 
-    for q in range(chunks):
-        @pl.when(is_source)
-        def _():
-            own_remote(q, 0).wait_send()
-            own_remote(q, 1).wait_send()
-
-        for unit in (ALONE, BOTH):
-            for upward in (True, False):
-                for step in range(hops(q, unit, upward)):
-                    hop(q, step, unit, upward).wait_send()
-        for distance in (-4, -3, -2, -1, 1, 2, 3):
-            y_copy(q, distance, ALONE).wait_send()
-            for unit in (ALONE, BOTH, FROM_Y):
-                pair_copy(q, distance, unit, core).wait_send()
-        for distance in (1, 2, 3):
-            to_owner(q, distance).wait_send()
-        when_not(here, lambda: to_owner(q, 0).wait_send())
-        across(q).wait_send()
-        agg_copy(q, core).wait_send()
-
-    @pl.when(jnp.logical_not(stays))
-    def _():
-        for i in range(PIECES + 1):
-            set_remote(i).wait_send()
-
-    slope_copy.wait_send()
     for step in FAR_FIRST:
-        grad_copy(step).wait_send()
         whole_copy(step).wait_send()
-    for distance in range(1, 16):
-        piece_copy(distance).wait_send()
-    for distance in near:
-        total_copy(distance).wait_send()
-    final.wait_send()
+    for n in range(16):
+        last_copy(n, core).wait_send()
 
 
 def shards(features, tiles, tile_rows, tile_cols, tile_count, weight, cotangent):

time: 125 us -> 121 us (0.968)
  Pallas kernels: 121 us -> 116 us
    pallas_call x1, Pallas kernels: 121 us -> 116 us  [shards(): pl.pallas_call(layer_kernel, out_shape=(jax.ShapeDtypeStruct(cotangent.sh...]
where the time goes in v4:
time: 121 us
  Pallas kernels  116 us (96%)
  other arithmetic  2.18 us (2%)
  between operations  1.29 us (1%)
    pallas_call x1, Pallas kernels, shards(): pl.pallas_call(layer_kernel, out_shape=(jax.ShapeDtypeStruct(cotangent.sh...  116 us

profile of v4, /device:TPU:1, one launch (start us, length us, event | category | flops | bytes accessed | tf_op | source)
XLA Modules:
  0.0 120.5 jit_solution(2478778896466947791)
XLA Ops:
  1.3 116.4 %layer.1 = (bf16[128,512]{1,0:T(8,128)(2,1)}, bf16[512,512]{1,0:T(8,128)(2,1)}) custom-call(bf16[8,128,512]{2,1,0:T(8,128)(2,1)} %bitcast.1, bf16[48,128,128]{2,1,0:T(8,128)(2,1)} %tiles_in.1, s32[48]{0:T(128)} %rows.1, s32[48]{0:T(128)} %cols.1, s32[1]{0:T(128)S(6)} %copy.10.count, bf16[512,512]{1,0:T(8,128)(2,1)} %weight_in.1, bf16[128,512]{1,0:T(8,128)(2,1)} %cotangent_in.1), custom_call_target="tpu_custom_call" | custom-call | tf_op jit(solution)/shard_map/layer/pallas_call | solution.py:629
  117.7 0.0 copy-start
  117.7 2.2 %convert_element_type.3 = f32[512,512]{1,0:T(8,128)} convert(bf16[512,512]{1,0:T(8,128)(2,1)} %get-tuple-element.5) | non-fusion elementwise | flops 262144 | bytes 1572864 | tf_op jit(solution)/shard_map/convert_element_type | solution.py:645
  119.9 0.0 copy-done
  119.9 0.7 copy.11
Async XLA Ops:
  117.7 2.2 %copy-start = (bf16[128,512]{1,0:T(8,128)(2,1)S(1)}, bf16[128,512]{1,0:T(8,128)(2,1)}, u32[]{:S(2)}) copy-start(bf16[128,512]{1,0:T(8,128)(2,1)} %get-tuple-element.8) | copy-start | bytes 393220

commit v5 on v4

--- a/solution.py
+++ b/solution.py
@@ -367,9 +367,9 @@
 
         lax.fori_loop(0, SLOT_STEP // 4, four, 0)
 
-    def multiplies(q, pieces):
-        slots = range(pieces[0] * per_piece, (pieces[-1] + 1) * per_piece, SLOT_STEP)
-        return [lambda first=first: multiply(q, first) for first in slots]
+    def multiply_pieces(q, piece):
+        for first in range(piece * per_piece, (piece + 1) * per_piece, SLOT_STEP):
+            multiply(q, first)
 
     set_x, set_y = set_of(x, y, zh, core)
     here = (set_x + 4 - x) % 4 == 0
@@ -480,32 +480,29 @@
         load.start()
     for q in range(chunks):
         of("products", q)[0] = jnp.zeros((128, WIDTHS[q]), F32)
-    work = []
     for slot, events in enumerate(slots, 1):
-        complete = slot // 2 - 3
         if slot in (2, 4, 6):
             greeted(slot // 2 - 1)
             if slot < 6:
                 greet(slot // 2)
         if slot == 6:
-            work += [lambda: pair_arrivals(0), receive_table, lambda: receive_piece(0)] + multiplies(0, (0,))
-            work += [lambda: receive_piece(1)] + multiplies(0, (1,))
-        elif slot % 2 == 0 and 0 < complete < chunks - 1:
-            work += [lambda q=complete: pair_arrivals(q)] + multiplies(complete, (0, 1))
+            pair_arrivals(0)
+            receive_table()
+            for piece in (0, 1):
+                receive_piece(piece)
+                multiply_pieces(0, piece)
+        if slot == 7:
+            receive_piece(2)
+            multiply_pieces(0, 2)
+            send_sums(0)
         for event in events:
             event()
-            if work:
-                work.pop(0)()
-    for item in work:
-        item()
-    receive_piece(2)
-    for q in range(chunks - 1):
-        for item in multiplies(q, (2,)):
-            item()
-        send_sums(q)
-    pair_arrivals(chunks - 1)
-    for item in multiplies(chunks - 1, (0, 1, 2)):
-        item()
+    for q in range(1, chunks):
+        pair_arrivals(q)
+        for piece in range(PIECES):
+            multiply_pieces(q, piece)
+        if q < chunks - 1:
+            send_sums(q)
     send_sums(chunks - 1)
     for q in range(chunks):
         drain_features(q)

time: 121 us -> 119 us (0.983)
    pallas_call x1, Pallas kernels: 116 us -> 115 us  [shards(): pl.pallas_call(layer_kernel, out_shape=(jax.ShapeDtypeStruct(cotangent.sh...]
where the time goes in v5:
time: 119 us
  Pallas kernels  115 us (97%)
  other arithmetic  2.18 us (2%)
  between operations  1.29 us (1%)
    pallas_call x1, Pallas kernels, shards(): pl.pallas_call(layer_kernel, out_shape=(jax.ShapeDtypeStruct(cotangent.sh...  115 us

profile of v5, /device:TPU:1, one launch (start us, length us, event | category | flops | bytes accessed | tf_op | source)
XLA Modules:
  0.0 119.1 jit_solution(13056452404460562591)
XLA Ops:
  1.3 115.0 %layer.1 = (bf16[128,512]{1,0:T(8,128)(2,1)}, bf16[512,512]{1,0:T(8,128)(2,1)}) custom-call(bf16[8,128,512]{2,1,0:T(8,128)(2,1)} %bitcast.1, bf16[48,128,128]{2,1,0:T(8,128)(2,1)} %tiles_in.1, s32[48]{0:T(128)} %rows.1, s32[48]{0:T(128)} %cols.1, s32[1]{0:T(128)S(6)} %copy.10.count, bf16[512,512]{1,0:T(8,128)(2,1)} %weight_in.1, bf16[128,512]{1,0:T(8,128)(2,1)} %cotangent_in.1), custom_call_target="tpu_custom_call" | custom-call | tf_op jit(solution)/shard_map/layer/pallas_call | solution.py:626
  116.3 0.0 copy-start
  116.3 2.2 %convert_element_type.3 = f32[512,512]{1,0:T(8,128)} convert(bf16[512,512]{1,0:T(8,128)(2,1)} %get-tuple-element.5) | non-fusion elementwise | flops 262144 | bytes 1572864 | tf_op jit(solution)/shard_map/convert_element_type | solution.py:642
  118.5 0.0 copy-done
  118.5 0.7 copy.11
Async XLA Ops:
  116.3 2.2 %copy-start = (bf16[128,512]{1,0:T(8,128)(2,1)S(1)}, bf16[128,512]{1,0:T(8,128)(2,1)}, u32[]{:S(2)}) copy-start(bf16[128,512]{1,0:T(8,128)(2,1)} %get-tuple-element.8) | copy-start | bytes 393220

commit v6 on v5

--- a/solution.py
+++ b/solution.py
@@ -193,12 +193,12 @@
     load_tiles = pltpu.make_async_copy(tiles_in, s.tiles, s.local_sems.at[0])
     load_tiles.start()
 
+    for step in FAR_FIRST:
+        signal(in_plane(step))
     signal(up)
     signal(down)
+    signal(y_pair_other)
     signal(sibling)
-    signal(y_pair_other)
-    for step in FAR_FIRST:
-        signal(in_plane(step))
     def entry(table, row, place, top):
         return jnp.minimum(jnp.maximum(table[row, place], 0), top)
 

time: 119 us -> 119 us (level)
  no operation moved by 1% of the time
where the time goes in v6:
time: 119 us
  Pallas kernels  115 us (97%)
  other arithmetic  2.18 us (2%)
  between operations  1.29 us (1%)
    pallas_call x1, Pallas kernels, shards(): pl.pallas_call(layer_kernel, out_shape=(jax.ShapeDtypeStruct(cotangent.sh...  115 us

profile of v6, /device:TPU:1, one launch (start us, length us, event | category | flops | bytes accessed | tf_op | source)
XLA Modules:
  0.0 119.1 jit_solution(12130506879178311629)
XLA Ops:
  1.3 115.0 %layer.1 = (bf16[128,512]{1,0:T(8,128)(2,1)}, bf16[512,512]{1,0:T(8,128)(2,1)}) custom-call(bf16[8,128,512]{2,1,0:T(8,128)(2,1)} %bitcast.1, bf16[48,128,128]{2,1,0:T(8,128)(2,1)} %tiles_in.1, s32[48]{0:T(128)} %rows.1, s32[48]{0:T(128)} %cols.1, s32[1]{0:T(128)S(6)} %copy.10.count, bf16[512,512]{1,0:T(8,128)(2,1)} %weight_in.1, bf16[128,512]{1,0:T(8,128)(2,1)} %cotangent_in.1), custom_call_target="tpu_custom_call" | custom-call | tf_op jit(solution)/shard_map/layer/pallas_call | solution.py:626
  116.3 0.0 copy-start
  116.3 2.2 %convert_element_type.3 = f32[512,512]{1,0:T(8,128)} convert(bf16[512,512]{1,0:T(8,128)(2,1)} %get-tuple-element.5) | non-fusion elementwise | flops 262144 | bytes 1572864 | tf_op jit(solution)/shard_map/convert_element_type | solution.py:642
  118.5 0.0 copy-done
  118.5 0.7 copy.11
Async XLA Ops:
  116.3 2.2 %copy-start = (bf16[128,512]{1,0:T(8,128)(2,1)S(1)}, bf16[128,512]{1,0:T(8,128)(2,1)}, u32[]{:S(2)}) copy-start(bf16[128,512]{1,0:T(8,128)(2,1)} %get-tuple-element.8) | copy-start | bytes 393220
